TPU v7x, 32 devices: a whole 2x2x4 slice. The times are simulated.
32 devices in a mesh: dp: 8 (over y, x, core), tensor: 4 (over z).
Axes of the slice: x: 2, y: 2, z: 4, core: 2. Of those that a mesh axis runs over, the one named last changes fastest.
Arguments:
- tokens: bfloat16 [8192, 768], P('dp'), may hold values from -6 to 6
- segments: int32 [8, 1024], P('dp'), may hold values from 0 to 3, as said below
- routes: int32 [8192, 2], P('dp'), may hold values from 0 to 3, all different within a row; in each aligned block of 1024 rows (0 to 1023, 1024 to 2047, ...) at most 704 rows name the same one
- grad_out: bfloat16 [8192, 768], P('dp'), may hold values from -6 to 6
- gain_attn: bfloat16 [768], replicated, may hold values from 0.5 to 1.5
- w_qkv: bfloat16 [3, 768, 768], P(None, None, 'tensor'), may hold values from -0.21875 to 0.21875
- w_out: bfloat16 [768, 768], P('tensor'), may hold values from -0.875 to 0.875
- rel_bias: bfloat16 [32, 12], P(None, 'tensor'), may hold values from -4 to 4
- gain_moe: bfloat16 [768], replicated, may hold values from 0.5 to 1.5
- w_router: bfloat16 [768, 4], replicated, may hold values from -0.15625 to 0.15625
- w_in: bfloat16 [4, 768, 3072], P(None, None, 'tensor'), may hold values from -0.21875 to 0.21875
- w_down: bfloat16 [4, 3072, 768], P(None, 'tensor'), may hold values from -0.15625 to 0.15625
Outputs:
- result: bfloat16 [8192, 768], P('dp')
- grad_tokens: float32 [8192, 768], P('dp')
- grad_gain_attn: float32 [768], replicated
- grad_w_qkv: float32 [3, 768, 768], P(None, None, 'tensor')
- grad_w_out: float32 [768, 768], P('tensor')
- grad_rel_bias: float32 [32, 12], P(None, 'tensor')
- grad_gain_moe: float32 [768], replicated
- grad_w_router: float32 [768, 4], replicated
- grad_w_in: float32 [4, 768, 3072], P(None, None, 'tensor')
- grad_w_down: float32 [4, 3072, 768], P(None, 'tensor')
Inputs may be any that keep to these rules, and one draw needn't show every extreme that they name: `routes`: the two experts of a token differ. Among the 1024 rows of one index of dp no expert is named more than 704 times, a bound that some block reaches. `segments`: document numbers start at 0 and rise by one at each document's end; a sequence holds 2 to 4 documents, each of 204 positions or more.
All inputs are finite; a program needn't handle non-finite values.
Results may differ from a plain program's by a relative error of at most 0.017.
Values may be sent and summed in bfloat16 or wider, within the bound.
No kernel may reach another device: no remote copies, remote signals or barrier semaphores. Data moves between devices by JAX's collectives and lax.ppermute only.
A program may use at most 192 MiB of HBM per device.

v0:
```python
import math

import jax
import jax.numpy as jnp
from jax import lax
from jax.sharding import PartitionSpec as P

NB = 32
DIST = 128
CAP = 704


EPSILON = 1e-06
NEGATIVE = -1e30
HIGHEST = lax.Precision.HIGHEST


def bucket_ids(distance):
    halfway = NB // 2
    thresholds = [
        int(math.ceil(halfway * (DIST / halfway) ** (step / halfway))) for step in range(halfway)
    ]
    beyond = jnp.zeros_like(distance)
    for threshold in thresholds:
        beyond = beyond + (distance >= threshold).astype(jnp.int32)
    return jnp.where(distance < halfway, distance, halfway - 1 + beyond)


def gelu_tanh(values):
    inner_arg = 0.7978845608028654 * (values + 0.044715 * values * values * values)
    return 0.5 * values * (1.0 + jnp.tanh(inner_arg))


def rms_scale(values):
    return lax.rsqrt(jnp.mean(values * values, axis=-1, keepdims=True) + EPSILON)


def norm_back(grad_normed, inputs, row_scale, gain_vector):
    normalized = inputs * row_scale
    gained = grad_normed * gain_vector
    grad_gain = jnp.sum(grad_normed * normalized, axis=0)
    grad_inputs = row_scale * (
        gained - normalized * jnp.mean(gained * normalized, axis=-1, keepdims=True)
    )
    return (grad_inputs, grad_gain)


def body(
    tokens,
    segments,
    routes,
    grad_out,
    gain_attn,
    w_qkv,
    w_out,
    rel_bias,
    gain_moe,
    w_router,
    w_in,
    w_down,
):
    tok_rows, model_width = tokens.shape
    seq_count, seq_len = segments.shape
    heads_local = rel_bias.shape[1]
    features = w_qkv.shape[2]
    head_size = features // heads_local
    experts = w_in.shape[0]
    block_rows = min(512, seq_len)
    per_seq = seq_len // block_rows
    block_count = seq_count * per_seq
    inv_root = head_size ** (-0.5)
    inputs = tokens.astype(jnp.float32)
    gain_one = gain_attn.astype(jnp.float32)
    gain_two = gain_moe.astype(jnp.float32)
    scale_one = rms_scale(inputs)
    normed_one = (inputs * scale_one * gain_one).astype(jnp.bfloat16)
    projected = jnp.einsum(
        "td,cdf->ctf", normed_one, w_qkv, preferred_element_type=jnp.float32
    ).astype(jnp.bfloat16)
    positions = jnp.arange(seq_len)

    def block_scores(block_index):
        seq_index = block_index // per_seq
        seq_start = seq_index * seq_len
        row_start = block_index % per_seq * block_rows
        query_block = lax.dynamic_slice_in_dim(
            projected[0], seq_start + row_start, block_rows, 0
        ).reshape(block_rows, heads_local, head_size)
        key_block = projected[1].reshape(seq_len, heads_local, head_size)
        value_block = projected[2].reshape(seq_len, heads_local, head_size)
        seg_row = lax.dynamic_index_in_dim(segments, seq_index, 0, keepdims=False)
        row_ids = row_start + jnp.arange(block_rows)
        distance = row_ids[:, None] - positions[None, :]
        bucket_block = bucket_ids(jnp.maximum(distance, 0))
        bucket_mask = (bucket_block[:, :, None] == jnp.arange(NB)[None, None, :]).astype(
            jnp.bfloat16
        )
        seg_block = lax.dynamic_slice_in_dim(seg_row, row_start, block_rows, 0)
        allowed = (distance >= 0) & (seg_block[:, None] == seg_row[None, :])
        raw_scores = jnp.einsum(
            "qhe,khe->hqk", query_block, key_block, preferred_element_type=jnp.float32
        )
        bias_block = jnp.einsum(
            "bh,qkb->hqk", rel_bias, bucket_mask, preferred_element_type=jnp.float32
        )
        scores = jnp.where(allowed[None], raw_scores * inv_root + bias_block, NEGATIVE)
        return (scores, bucket_mask, query_block, key_block, value_block)

    def forward_block(block_index):
        scores, bucket_mask, query_block, key_block, value_block = block_scores(block_index)
        row_peak = jnp.max(scores, axis=-1, keepdims=True)
        raised = jnp.exp(scores - row_peak)
        row_total = jnp.sum(raised, axis=-1, keepdims=True)
        prob_block = raised / row_total
        mixed_block = jnp.einsum(
            "hqk,khe->qhe",
            prob_block.astype(jnp.bfloat16),
            value_block,
            preferred_element_type=jnp.float32,
        )
        return (
            mixed_block.reshape(block_rows, features).astype(jnp.bfloat16),
            (row_peak + jnp.log(row_total))[:, :, 0],
        )

    attended, log_totals = lax.map(forward_block, jnp.arange(block_count))
    attended = attended.reshape(tok_rows, features)
    attn_part = jnp.dot(attended, w_out, preferred_element_type=jnp.float32)
    attn_sum = lax.psum(attn_part, "tensor")
    hidden_one = inputs + attn_sum
    scale_two = rms_scale(hidden_one)
    normed_two = (hidden_one * scale_two * gain_two).astype(jnp.bfloat16)
    logits = jnp.dot(normed_two, w_router, preferred_element_type=jnp.float32)
    chosen = jnp.take_along_axis(logits, routes, axis=1)
    row_peak = jnp.max(chosen, axis=1, keepdims=True)
    raised = jnp.exp(chosen - row_peak)
    gate_values = raised / jnp.sum(raised, axis=1, keepdims=True)
    flat_routes = routes.reshape(-1)
    pair_count = flat_routes.shape[0]
    one_hot = (flat_routes[:, None] == jnp.arange(experts)[None, :]).astype(jnp.int32)
    earlier = jnp.cumsum(one_hot, axis=0) - one_hot
    position = flat_routes * CAP + jnp.sum(earlier * one_hot, axis=1)
    slot_owner = (
        jnp.full((experts * CAP,), pair_count, jnp.int32)
        .at[position]
        .set(jnp.arange(pair_count, dtype=jnp.int32))
    )
    padded_rows = jnp.concatenate([normed_two, jnp.zeros((1, model_width), jnp.bfloat16)], axis=0)
    buffer = padded_rows[slot_owner // 2].reshape(experts, CAP, model_width)
    pre_act = jnp.einsum("ecd,edf->ecf", buffer, w_in, preferred_element_type=jnp.float32)
    activated = gelu_tanh(pre_act).astype(jnp.bfloat16)
    expert_out = jnp.einsum(
        "ecf,efd->ecd", activated, w_down, preferred_element_type=jnp.float32
    ).reshape(experts * CAP, model_width)
    picked = expert_out[position].reshape(tok_rows, 2, model_width)
    moe_part = jnp.sum(gate_values[:, :, None] * picked, axis=1)
    row_share = tok_rows // lax.axis_size("tensor")
    moe_rows = lax.psum_scatter(
        moe_part.astype(jnp.bfloat16), "tensor", scatter_dimension=0, tiled=True
    ).astype(jnp.float32)
    hidden_rows = lax.dynamic_slice_in_dim(
        hidden_one, lax.axis_index("tensor") * row_share, row_share, 0
    )
    result_share = (hidden_rows + moe_rows).astype(jnp.bfloat16)
    result = lax.all_gather(result_share, "tensor", axis=0, tiled=True)
    cotangent = grad_out.astype(jnp.float32)
    grad_gate = jnp.sum(cotangent[:, None, :] * picked, axis=2)
    contrib = (
        (gate_values[:, :, None] * cotangent[:, None, :])
        .reshape(pair_count, model_width)
        .astype(jnp.bfloat16)
    )
    contrib = jnp.concatenate([contrib, jnp.zeros((1, model_width), jnp.bfloat16)], axis=0)
    grad_expert = contrib[slot_owner].reshape(experts, CAP, model_width)
    grad_w_down = jnp.einsum(
        "ecf,ecd->efd", activated, grad_expert, preferred_element_type=jnp.float32
    )
    grad_act = jnp.einsum("ecd,efd->ecf", grad_expert, w_down, preferred_element_type=jnp.float32)
    gelu_pull = jax.vjp(gelu_tanh, pre_act)[1]
    grad_pre = gelu_pull(grad_act)[0].astype(jnp.bfloat16)
    grad_w_in = jnp.einsum("ecd,ecf->edf", buffer, grad_pre, preferred_element_type=jnp.float32)
    grad_buffer = jnp.einsum(
        "ecf,edf->ecd", grad_pre, w_in, preferred_element_type=jnp.float32
    ).reshape(experts * CAP, model_width)
    grad_normed_part = jnp.sum(grad_buffer[position].reshape(tok_rows, 2, model_width), axis=1)
    mean_gate = jnp.sum(gate_values * grad_gate, axis=1, keepdims=True)
    grad_chosen = gate_values * (grad_gate - mean_gate)
    grad_logit_part = jnp.sum(
        one_hot.reshape(tok_rows, 2, experts).astype(jnp.float32) * grad_chosen[:, :, None], axis=1
    )
    grad_normed_sum, grad_logits = lax.psum((grad_normed_part, grad_logit_part), "tensor")
    grad_normed_two = grad_normed_sum + jnp.dot(
        grad_logits, w_router.astype(jnp.float32).T, precision=HIGHEST
    )
    grad_router_rows = jnp.dot(grad_logits.T, normed_two.astype(jnp.float32), precision=HIGHEST)
    grad_hidden_norm, grad_gain_two = norm_back(grad_normed_two, hidden_one, scale_two, gain_two)
    grad_hidden = cotangent + grad_hidden_norm
    grad_hidden_low = grad_hidden.astype(jnp.bfloat16)
    grad_w_out = jnp.dot(attended.T, grad_hidden_low, preferred_element_type=jnp.float32)
    grad_attended = jnp.dot(grad_hidden_low, w_out.T, preferred_element_type=jnp.float32).astype(
        jnp.bfloat16
    )

    def backward_block(running, block_index):
        grad_keys, grad_values, grad_bias = running
        scores, bucket_mask, query_block, key_block, value_block = block_scores(block_index)
        seq_start = block_index // per_seq * seq_len
        row_start = seq_start + block_index % per_seq * block_rows
        log_total = lax.dynamic_index_in_dim(log_totals, block_index, 0, keepdims=False)
        prob_block = jnp.exp(scores - log_total[:, :, None])
        grad_block = lax.dynamic_slice_in_dim(grad_attended, row_start, block_rows, 0).reshape(
            block_rows, heads_local, head_size
        )
        grad_probs = jnp.einsum(
            "qhe,khe->hqk", grad_block, value_block, preferred_element_type=jnp.float32
        )
        grad_scores = prob_block * (
            grad_probs - jnp.sum(prob_block * grad_probs, axis=-1, keepdims=True)
        )
        grad_bias = grad_bias + jnp.einsum(
            "hqk,qkb->bh", grad_scores, bucket_mask.astype(jnp.float32), precision=HIGHEST
        )
        grad_raw = (grad_scores * inv_root).astype(jnp.bfloat16)
        grad_query = jnp.einsum(
            "hqk,khe->qhe", grad_raw, key_block, preferred_element_type=jnp.float32
        )
        key_part = jnp.einsum(
            "hqk,qhe->khe", grad_raw, query_block, preferred_element_type=jnp.float32
        ).reshape(seq_len, features)
        value_part = jnp.einsum(
            "hqk,qhe->khe",
            prob_block.astype(jnp.bfloat16),
            grad_block,
            preferred_element_type=jnp.float32,
        ).reshape(seq_len, features)
        grad_keys = grad_keys + key_part
        grad_values = grad_values + value_part
        return (
            (grad_keys, grad_values, grad_bias),
            grad_query.reshape(block_rows, features).astype(jnp.bfloat16),
        )

    zero_rows = jnp.zeros((tok_rows, features), jnp.float32)
    initial = (zero_rows, zero_rows, jnp.zeros((NB, heads_local), jnp.float32))
    (grad_keys, grad_values, grad_rel), grad_queries = lax.scan(
        backward_block, initial, jnp.arange(block_count)
    )
    grad_projected = jnp.stack(
        [
            grad_queries.reshape(tok_rows, features),
            grad_keys.astype(jnp.bfloat16),
            grad_values.astype(jnp.bfloat16),
        ]
    )
    grad_w_qkv = jnp.einsum(
        "td,ctf->cdf", normed_one, grad_projected, preferred_element_type=jnp.float32
    )
    grad_normed_one_part = jnp.einsum(
        "ctf,cdf->td", grad_projected, w_qkv, preferred_element_type=jnp.float32
    )
    grad_normed_one = lax.psum(grad_normed_one_part.astype(jnp.bfloat16), "tensor").astype(
        jnp.float32
    )
    grad_input_norm, grad_gain_one = norm_back(grad_normed_one, inputs, scale_one, gain_one)
    grad_tokens = grad_hidden + grad_input_norm
    rel_flat = jnp.pad(grad_rel.reshape(-1), (0, model_width - NB * heads_local))
    small_rows = jnp.concatenate(
        [grad_gain_one[None], grad_gain_two[None], rel_flat[None], grad_router_rows], axis=0
    )
    reduced_qkv, reduced_out, reduced_in, reduced_down, reduced_small = (
        lax.psum_scatter(grad_w_qkv, "dp", scatter_dimension=1, tiled=True),
        lax.psum_scatter(grad_w_out, "dp", scatter_dimension=1, tiled=True),
        lax.psum_scatter(grad_w_in, "dp", scatter_dimension=1, tiled=True),
        lax.psum_scatter(grad_w_down, "dp", scatter_dimension=2, tiled=True),
        lax.psum_scatter(small_rows, "dp", scatter_dimension=1, tiled=True),
    )
    grad_w_qkv, grad_w_out, grad_w_in, grad_w_down, small_rows = (
        lax.all_gather(reduced_qkv.astype(jnp.bfloat16), "dp", axis=1, tiled=True).astype(
            reduced_qkv.dtype
        ),
        lax.all_gather(reduced_out.astype(jnp.bfloat16), "dp", axis=1, tiled=True).astype(
            reduced_out.dtype
        ),
        lax.all_gather(reduced_in.astype(jnp.bfloat16), "dp", axis=1, tiled=True).astype(
            reduced_in.dtype
        ),
        lax.all_gather(reduced_down.astype(jnp.bfloat16), "dp", axis=2, tiled=True).astype(
            reduced_down.dtype
        ),
        lax.all_gather(reduced_small.astype(jnp.bfloat16), "dp", axis=1, tiled=True).astype(
            reduced_small.dtype
        ),
    )
    grad_gain_attn = small_rows[0]
    grad_gain_moe = small_rows[1]
    grad_rel_bias = small_rows[2, : NB * heads_local].reshape(NB, heads_local)
    grad_w_router = small_rows[3:].T
    return (
        result,
        grad_tokens,
        grad_gain_attn,
        grad_w_qkv,
        grad_w_out,
        grad_rel_bias,
        grad_gain_moe,
        grad_w_router,
        grad_w_in,
        grad_w_down,
    )


def solution(mesh):
    placed = (
        P("dp", None),
        P("dp", None),
        P("dp", None),
        P("dp", None),
        P(),
        P(None, None, "tensor"),
        P("tensor", None),
        P(None, "tensor"),
        P(),
        P(),
        P(None, None, "tensor"),
        P(None, "tensor", None),
    )
    return jax.shard_map(
        body,
        mesh=mesh,
        in_specs=placed,
        out_specs=(
            P("dp", None),
            P("dp", None),
            P(),
            P(None, None, "tensor"),
            P("tensor", None),
            P(None, "tensor"),
            P(),
            P(),
            P(None, None, "tensor"),
            P(None, "tensor", None),
        ),
        check_vma=False,
    )
```

profile of v0, /device:TPU:0, one launch (start us, length us, event | category | flops | bytes accessed | tf_op | source)
XLA Modules:
  0.0 1183.8 jit_solution(3122283884862144722)
XLA Ops:
  13.2 52.8 %while.34 = (s32[]{:T(128)}, bf16[2,512,192]{1,2,0:T(8,128)(2,1)S(1)}, f32[2,3,512]{2,1,0:T(4,128)S(1)}, s32[2]{0:T(128)S(1)}, s32[1,1024]{1,0:T(1,128)S(1)}, /*...) while((s32[]{:T(128)}, ...), condition=%wide.region_4.5_spmd.clone, body=%wide.region_1.4_spmd.clone.sunk | while | flops 563706880 | bytes 41097864 | solution.py:126
  20.9 10.2 fusion.188
  47.1 10.2 fusion.188
  95.2 98.0 %all-reduce.7.cloned.1.call-done = f32[1024,768]{1,0:T(8,128)} async-done(((f32[1024,768]{1,0:T(8,128)}), f32[1024,768]{1,0:T(8,128)}) %all-reduce.7.cloned.1.call-update) | async-done | bytes 3145744 | tf_op jit(solution)/shard_map/psum | solution.py:129
  199.3 17.8 %gather_fusion.4 = f32[2048]{0:T(1024)S(1)} fusion(f32[1024,4]{0,1:T(4,128)S(1)} %fusion.117, s32[2048]{0:T(1024)S(1)} %reshape.631), kind=kCustom, calls=%fused_computation.4 | custom fusion | bytes 32768 | tf_op jit(solution)/shard_map/jit(take_along_axis)/gather | solution.py:134
  234.3 13.5 %gather_fusion.2 = bf16[2816,768]{1,0:T(8,128)(2,1)} fusion(bf16[2049,768]{1,0:T(8,128)(2,1)} %concatenate.10, s32[3072]{0:T(1024)S(1)} %copy-done.42), kind=kCustom, calls=%fused_computation.2 | custom fusion | bytes 8662016 | tf_op jit(solution)/shard_map/gather | solution.py:174
  254.7 16.0 %fusion.70 = (bf16[4,704,768]{2,1,0:T(8,128)(2,1)}, f32[4,704,768]{2,1,0:T(8,128)}) fusion(f32[4,704,768]{2,1,0:T(8,128)S(1)} %fusion.118, bf16[4,704,768]{2,1,0:T(8,128)(2,1)} %bitcast.245, bf16[4,768,768]{2,1,0:T(8,128)(2,1)} %param.26), kind=kOutput, calls=%fused_computation.103 | convolution fusion | flops 3373793280 | bytes 30670848 | tf_op jit(solution)/shard_map/ecd,edf->ecf/dot_general | solution.py:150
  280.0 14.0 %gather_fusion.3 = f32[2048,768]{1,0:T(8,128)} fusion(f32[2816,768]{1,0:T(8,128)} %bitcast.229, s32[2048]{0:T(1024)S(1)} %copy-done.37), kind=kCustom, calls=%fused_computation.3 | custom fusion | bytes 12591104 | tf_op jit(solution)/shard_map/gather | solution.py:185
  302.4 12.0 %reduce_sum.149 = f32[1024,768]{1,0:T(8,128)} reduce(f32[1024,2,768]{2,1,0:T(2,128)} %reshape.597, f32[]{:T(128)} %constant.402.clone.1), dimensions={1}, to_apply=%region_15.16 | reduce | flops 786432 | bytes 9437188 | tf_op jit(solution)/shard_map/reduce_sum | solution.py:185
  317.7 12.8 %fusion.109 = f32[4,704,768]{2,1,0:T(8,128)} fusion(bf16[4,768,768]{2,1,0:T(8,128)(2,1)} %param.27, f32[4,704,768]{2,1,0:T(8,128)} %get-tuple-element.453), kind=kOutput, calls=%fused_computation.195 | convolution fusion | flops 3341352960 | bytes 22020096 | tf_op jit(solution)/shard_map/ecf,efd->ecd/dot_general | solution.py:152
  330.5 14.5 %gather_fusion.1 = f32[2048,768]{1,0:T(8,128)} fusion(f32[2816,768]{1,0:T(8,128)} %bitcast.228, s32[2048]{0:T(1024)S(1)} %copy-done.37), kind=kCustom, calls=%fused_computation.1 | custom fusion | bytes 12591104 | tf_op jit(solution)/shard_map/gather | solution.py:155
  353.2 16.8 %multiply_reduce_fusion.1 = (f32[1024,2]{1,0:T(8,128)S(1)}, bf16[1024,768]{1,0:T(8,128)(2,1)}) fusion(f32[1024,2,768]{2,1,0:T(2,128)} %reshape.594, f32[1024,768]{1,0:T(8,128)} %convert_element_type.499, f32[1024,2]{1,0:T(8,128)S(1)} %copy.128), kind=kLoop, calls=%fused_computation.108 | loop fusion | flops 5502976 | bytes 11026432 | tf_op jit(solution)/shard_map/reduce_sum | solution.py:167
  370.3 16.7 %psum.30 = f32[1024,4]{0,1:T(4,128)S(1)} all-reduce(f32[1024,4]{0,1:T(4,128)S(1)} %multiply_reduce_fusion.6), channel_id=1, replica_groups=mesh['dp'=8,'tensor'=4] {'tensor'}, use_global_device_ids=true, to_apply=%region_20.21 | all-reduce | flops 4096 | bytes 32768 | tf_op jit(solution)/shard_map/psum | solution.py:191
  387.0 47.7 %all-reduce.9.cloned.1.call-done = f32[1024,768]{1,0:T(8,128)} async-done(((f32[1024,768]{1,0:T(8,128)}), f32[1024,768]{1,0:T(8,128)}) %all-reduce.9.cloned.1.call-update) | async-done | bytes 3145744 | tf_op jit(solution)/shard_map/psum | solution.py:191
  445.9 212.1 %while.35 = (s32[]{:T(128)}, f32[1024,192]{0,1:T(8,128)}, f32[1024,192]{0,1:T(8,128)}, f32[32,3]{0,1:T(4,128)S(1)}, bf16[2,512,192]{1,2,0:T(8,128)(2,1)}, /*inde...) while((s32[]{:T(128)}, f32[1024,192]{0,1:T(8,128)}, ...), condition=%wide.region_24.25_spmd.clone, body=%wide.region_22.24_spmd.clone.sunk | while | flops 1795521792 | bytes 195542816 | solution.py:245
  465.8 11.7 fusion.205
  518.0 33.9 %fusion.209 = f32[32,3]{0,1:T(4,128)S(1)} fusion(f32[3,512,1024]{1,0,2:T(4,128)} %copy.160, s32[512,1024]{0,1:T(8,128)} %copy.158, f32[32,3]{0,1:T(4,128)S(1)} %get-tuple-element.650, pred[]{:T(512)S(6)} %compare.22), kind=kOutput, calls=%fused_computation.84.clone.1 | convolution fusion | flops 620757184 | bytes 8389377 | tf_op jit(solution)/shard_map/while/body/eval_jaxpr/hqk,qkb->bh/dot_general | solution.py:220
  571.5 11.7 fusion.205
  623.8 33.9 %fusion.209 = f32[32,3]{0,1:T(4,128)S(1)} fusion(f32[3,512,1024]{1,0,2:T(4,128)} %copy.160, s32[512,1024]{0,1:T(8,128)} %copy.158, f32[32,3]{0,1:T(4,128)S(1)} %get-tuple-element.650, pred[]{:T(512)S(6)} %compare.22), kind=kOutput, calls=%fused_computation.84.clone.1 | convolution fusion | flops 620757184 | bytes 8389377 | tf_op jit(solution)/shard_map/while/body/eval_jaxpr/hqk,qkb->bh/dot_general | solution.py:220
  664.3 11.2 fusion.121
  675.6 11.4 fusion.107
  694.1 37.9 %all-reduce.11.cloned.1.call-done = bf16[1024,768]{1,0:T(8,128)(2,1)} async-done(((bf16[1024,768]{1,0:T(8,128)(2,1)}), bf16[1024,768]{1,0:T(8,128)(2,1)}) %all-reduce.11.cloned.1.call-update) | async-done | bytes 1572880 | tf_op jit(solution)/shard_map/psum | solution.py:261
  735.6 33.5 %reduce-scatter.13.cloned.1.call-done = bf16[256,768]{1,0:T(8,128)(2,1)} async-done(((bf16[1024,768]{1,0:T(8,128)(2,1)}), bf16[256,768]{1,0:T(8,128)(2,1)}) %reduce-scatter.13.cloned.1.call-update) | async-done | bytes 393232 | tf_op jit(solution)/shard_map/reduce_scatter | solution.py:158
  783.9 64.6 %reduce-scatter.15.cloned.1.call-done = f32[4,96,768]{2,1,0:T(8,128)} async-done(((f32[4,768,768]{2,1,0:T(8,128)}), f32[4,96,768]{2,1,0:T(8,128)}) %reduce-scatter.15.cloned.1.call-update) | async-done | bytes 1179664 | tf_op jit(solution)/shard_map/reduce_scatter | solution.py:273
  850.7 78.2 %reduce-scatter.17.cloned.1.call-done = f32[4,768,96]{1,2,0:T(8,128)} async-done(((f32[4,768,768]{1,2,0:T(8,128)}), f32[4,768,96]{1,2,0:T(8,128)}) %reduce-scatter.17.cloned.1.call-update) | async-done | bytes 1179664 | tf_op jit(solution)/shard_map/reduce_scatter | solution.py:274
  931.1 36.0 %reduce-scatter.23.cloned.1.call-done = f32[96,192]{1,0:T(8,128)} async-done(((f32[768,192]{1,0:T(8,128)}), f32[96,192]{1,0:T(8,128)}) %reduce-scatter.23.cloned.1.call-update) | async-done | bytes 73744
  983.6 20.4 %reduce-scatter.19.cloned.1.call-done = f32[96,7]{1,0:T(8,128)} async-done(((f32[768,7]{1,0:T(8,128)}), f32[96,7]{1,0:T(8,128)}) %reduce-scatter.19.cloned.1.call-update) | async-done | bytes 2704
  1015.8 26.9 %all-gather.5.cloned.1.call-done = bf16[1024,768]{1,0:T(8,128)(2,1)} async-done(((bf16[256,768]{1,0:T(8,128)(2,1)}), bf16[1024,768]{1,0:T(8,128)(2,1)}) %all-gather.5.cloned.1.call-update) | async-done | bytes 1572880 | tf_op jit(solution)/shard_map/all_gather | solution.py:165
  1042.7 42.4 %reduce-scatter.21.cloned.1.call-done = f32[96,576]{1,0:T(8,128)} async-done(((f32[768,576]{1,0:T(8,128)}), f32[96,576]{1,0:T(8,128)}) %reduce-scatter.21.cloned.1.call-update) | async-done | bytes 221200
  1086.6 12.1 %all_gather.20 = bf16[3,768,192]{2,0,1:T(4,128)(2,1)S(1)} all-gather(bf16[3,96,192]{2,0,1:T(4,128)(2,1)S(1)} %copy.138), channel_id=1, replica_groups=mesh['dp'=8,'tensor'=4] {'dp'}, dimensions={1}, use_global_device_ids=true | all-gather | bytes 995328 | tf_op jit(solution)/shard_map/all_gather | solution.py:278
  1100.9 25.9 %all-gather.7.cloned.1.call-done = bf16[4,768,768]{2,1,0:T(8,128)(2,1)} async-done(((bf16[4,96,768]{2,1,0:T(8,128)(2,1)}), bf16[4,768,768]{2,1,0:T(8,128)(2,1)}) %all-gather.7.cloned.1.call-update) | async-done | bytes 4718608 | tf_op jit(solution)/shard_map/all_gather | solution.py:284
  1133.6 34.5 %all-gather.9.cloned.1.call-done = bf16[4,768,768]{1,2,0:T(8,128)(2,1)} async-done(((bf16[4,768,96]{1,2,0:T(8,128)(2,1)}), bf16[4,768,768]{1,2,0:T(8,128)(2,1)}) %all-gather.9.cloned.1.call-update) | async-done | bytes 4718608 | tf_op jit(solution)/shard_map/all_gather | solution.py:287
  (338 shorter events, 327.9 us)
Async XLA Ops:
  7.2 186.0 %all-reduce.7.cloned.1.call-start = ((), (), s32[]{:S(2)}) async-start(), calls=%async_computation.6 | async-start | bytes 6291456 | tf_op jit(solution)/shard_map/psum | solution.py:129
  13.2 53.8 %copy-start.24 = (bf16[192,768]{1,0:T(8,128)(2,1)S(1)}, bf16[192,768]{1,0:T(8,128)(2,1)}, u32[]{:S(2)}) copy-start(bf16[192,768]{1,0:T(8,128)(2,1)} %param.22) | copy-start | bytes 884740
  69.2 365.5 %all-reduce.9.cloned.1.call-start = ((), (), s32[]{:S(2)}) async-start(), calls=%async_computation.9 | async-start | bytes 6291456 | tf_op jit(solution)/shard_map/psum | solution.py:191
  70.1 125.5 %copy-start.38 = (f32[768]{0:T(1024)}, f32[768]{0:T(1024)S(1)}, u32[]{:S(2)}) copy-start(f32[768]{0:T(1024)S(1)} %convert_element_type.491) | copy-start | bytes 9220
  76.9 116.3 %copy-start.16 = (bf16[1024,768]{1,0:T(8,128)(2,1)S(1)}, bf16[1024,768]{1,0:T(8,128)(2,1)}, u32[]{:S(2)}) copy-start(bf16[1024,768]{1,0:T(8,128)(2,1)} %param.16) | copy-start | bytes 4718596
  199.3 18.5 %copy-start.32 = (s32[1024,2]{0,1:T(2,128)S(1)}, s32[1024,2]{0,1:T(2,128)}, u32[]{:S(2)}) copy-start(s32[1024,2]{0,1:T(2,128)} %param.18) | copy-start | bytes 24580
  247.8 22.9 %slice-start.2 = ((s8[4718592]{0:T(1024)(128)(4,1)}), s8[4194304]{0:T(1024)(128)(4,1)S(1)}, s32[]{:S(2)}) async-start(s8[4718592]{0:T(1024)(128)(4,1)} %bitcast.267), calls=%async_computation.20 | async-start | bytes 8388608
  254.7 16.0 %slice-start.3 = ((s8[4718592]{0:T(1024)(128)(4,1)}), s8[524288]{0:T(1024)(128)(4,1)S(1)}, s32[]{:S(2)}) async-start(s8[4718592]{0:T(1024)(128)(4,1)} %bitcast.267), calls=%async_computation.21 | async-start | bytes 1048576
  314.4 417.6 %all-reduce.11.cloned.1.call-start = ((), (), s32[]{:S(2)}) async-start(), calls=%async_computation.10 | async-start | bytes 3145728 | tf_op jit(solution)/shard_map/psum | solution.py:261
  353.2 81.5 %copy-start.39 = (f32[768]{0:T(1024)S(1)}, f32[768]{0:T(1024)}, u32[]{:S(2)}) copy-start(f32[768]{0:T(1024)} %copy-done.38) | copy-start | bytes 9220
  353.2 81.5 %copy-start.41 = (f32[1024]{0:T(1024)S(1)}, f32[1024]{0:T(1024)}, u32[]{:S(2)}) copy-start(f32[1024]{0:T(1024)} %copy-done.40) | copy-start | bytes 12292
  387.0 54.2 %copy-start.33 = (f32[1024,4]{0,1:T(4,128)}, f32[1024,4]{0,1:T(4,128)S(1)}, u32[]{:S(2)}) copy-start(f32[1024,4]{0,1:T(4,128)S(1)} %psum.30) | copy-start | bytes 49156
  477.4 17.1 %slice-start = ((s8[6291456]{0:T(1024)(128)(4,1)}), s8[2097152]{0:T(1024)(128)(4,1)S(1)}, s32[]{:S(2)}) async-start(s8[6291456]{0:T(1024)(128)(4,1)} %bitcast.226), calls=%async_computation.18 | async-start | bytes 4194304 | tf_op jit(solution)/shard_map/while
  508.4 9.6 copy-start.12
  518.0 33.9 %copy-start.4 = (bf16[3,1024,192]{1,2,0:T(8,128)(2,1)S(1)}, bf16[3,1024,192]{1,2,0:T(8,128)(2,1)}, u32[]{:S(2)}) copy-start(bf16[3,1024,192]{1,2,0:T(8,128)(2,1)} %get-tuple-element.731) | copy-start | bytes 3538948 | tf_op jit(solution)/shard_map/while
  583.2 17.1 %slice-start = ((s8[6291456]{0:T(1024)(128)(4,1)}), s8[2097152]{0:T(1024)(128)(4,1)S(1)}, s32[]{:S(2)}) async-start(s8[6291456]{0:T(1024)(128)(4,1)} %bitcast.226), calls=%async_computation.18 | async-start | bytes 4194304 | tf_op jit(solution)/shard_map/while
  614.1 9.6 copy-start.12
  623.8 33.9 %copy-start.4 = (bf16[3,1024,192]{1,2,0:T(8,128)(2,1)S(1)}, bf16[3,1024,192]{1,2,0:T(8,128)(2,1)}, u32[]{:S(2)}) copy-start(bf16[3,1024,192]{1,2,0:T(8,128)(2,1)} %get-tuple-element.731) | copy-start | bytes 3538948 | tf_op jit(solution)/shard_map/while
  663.7 105.3 %reduce-scatter.13.cloned.1.call-start = ((), (), s32[]{:S(2)}) async-start(), calls=%async_computation.7 | async-start | bytes 1966080 | tf_op jit(solution)/shard_map/reduce_scatter | solution.py:158
  664.3 184.2 %reduce-scatter.15.cloned.1.call-start = ((), (), s32[]{:S(2)}) async-start(), calls=%async_computation.11 | async-start | bytes 10616832 | tf_op jit(solution)/shard_map/reduce_scatter | solution.py:273
  675.5 253.4 %reduce-scatter.17.cloned.1.call-start = ((), (), s32[]{:S(2)}) async-start(), calls=%async_computation.13 | async-start | bytes 10616832 | tf_op jit(solution)/shard_map/reduce_scatter | solution.py:274
  687.0 45.0 %copy-start.17 = (bf16[1024,768]{1,0:T(8,128)(2,1)S(1)}, bf16[1024,768]{1,0:T(8,128)(2,1)}, u32[]{:S(2)}) copy-start(bf16[1024,768]{1,0:T(8,128)(2,1)} %param.16) | copy-start | bytes 4718596
  687.0 44.9 %copy-start.45 = (f32[768]{0:T(1024)S(1)}, f32[768]{0:T(1024)}, u32[]{:S(2)}) copy-start(f32[768]{0:T(1024)} %copy-done.44) | copy-start | bytes 9220
  687.0 44.9 %copy-start.47 = (f32[1024]{0:T(1024)S(1)}, f32[1024]{0:T(1024)}, u32[]{:S(2)}) copy-start(f32[1024]{0:T(1024)} %copy-done.46) | copy-start | bytes 12292
  687.0 280.1 %reduce-scatter.23.cloned.1.call-start = ((), (), s32[]{:S(2)}) async-start(), calls=%async_computation.17 | async-start | bytes 884736
  691.5 312.5 %reduce-scatter.19.cloned.1.call-start = ((), (), s32[]{:S(2)}) async-start(), calls=%async_computation.15 | async-start | bytes 442368
  693.9 77.4 %copy-start.29 = (bf16[1,1024,192]{1,2,0:T(8,128)(2,1)S(1)}, bf16[1,1024,192]{1,2,0:T(8,128)(2,1)}, u32[]{:S(2)}) copy-start(bf16[1,1024,192]{1,2,0:T(8,128)(2,1)} %copy-done.28) | copy-start | bytes 1179652
  735.6 307.2 %all-gather.5.cloned.1.call-start = ((), (), s32[]{:S(2)}) async-start(), calls=%async_computation.8 | async-start | bytes 1966080 | tf_op jit(solution)/shard_map/all_gather | solution.py:165
  771.2 314.0 %reduce-scatter.21.cloned.1.call-start = ((), (), s32[]{:S(2)}) async-start(), calls=%async_computation.16 | async-start | bytes 2211840
  783.8 342.9 %all-gather.7.cloned.1.call-start = ((), (), s32[]{:S(2)}) async-start(), calls=%async_computation.12 | async-start | bytes 5308416 | tf_op jit(solution)/shard_map/all_gather | solution.py:284
  850.6 317.6 %all-gather.9.cloned.1.call-start = ((), (), s32[]{:S(2)}) async-start(), calls=%async_computation.14 | async-start | bytes 5308416 | tf_op jit(solution)/shard_map/all_gather | solution.py:287
  1133.6 42.0 %copy-start.23 = (bf16[1024,768]{1,0:T(8,128)(2,1)S(1)}, bf16[1024,768]{1,0:T(8,128)(2,1)}, u32[]{:S(2)}) copy-start(bf16[1024,768]{1,0:T(8,128)(2,1)} %all-gather.5.cloned.1.call-done) | copy-start | bytes 4718596
  (48 other events, 146.9 us)
Sparse Core Ops, SparseCore 0:
  69.3 123.7 all-reduce.6
  314.5 120.1 all-reduce.8
  663.8 68.0 all-reduce.10
  734.7 34.3 reduce-scatter.12
  773.0 75.4 reduce-scatter.14
  852.4 76.4 reduce-scatter.16
  932.1 34.9 reduce-scatter.22
  970.1 33.8 reduce-scatter.18
  1005.6 37.0 all-gather.4
  1046.0 39.1 reduce-scatter.20
  1087.8 38.8 all-gather.6
  1129.2 38.9 all-gather.8
where the time goes:
time: 1200 us; the launch traced here: 1180 us
  waiting for transfers between devices  547 us (46%)
  matrix products  258 us (22%)
  local copies, waits for them, and re-layouts  207 us (17%)
  other arithmetic  95.1 us (8%)
  blocking collectives  47.2 us (4%)
  between operations  15.2 us (1%)
  loops' own time  14.6 us (1%)
    unnamed x15, waiting for transfers between devices  99.6 us
    psum x1, waiting for transfers between devices, body(): attn_sum = lax.psum(attn_part, 'tensor')  98 us
    reduce_scatter x1, waiting for transfers between devices, body(): lax.psum_scatter(grad_w_down, 'dp', scatter_dimension=2, tiled=True)  78.2 us
    dot_general x2, matrix products, backward_block(): jnp.einsum('hqk,qkb->bh', grad_scores, bucket_mask.astype(jnp.float32), p...  67.7 us
    reduce_scatter x1, waiting for transfers between devices, body(): lax.psum_scatter(grad_w_in, 'dp', scatter_dimension=1, tiled=True)  64.6 us
    psum x1, waiting for transfers between devices, body(): lax.psum((grad_normed_part, grad_logit_part), 'tensor')  47.7 us
    dot_general x4, matrix products, block_scores(): jnp.einsum('bh,qkb->hqk', rel_bias, bucket_mask, preferred_element_type=j...  43.7 us
    psum x1, waiting for transfers between devices, body(): lax.psum(grad_normed_one_part.astype(jnp.bfloat16), 'tensor')  37.9 us
  transfers between devices with their start and end apart: 12, of which 12 were waited for; matrix products, arithmetic and copies ran while one was open for 13% of the time, Pallas kernels for 0%

commit v1 on v0

v1 whole, which is shorter than its diff:
```python
import functools
import math

import jax
import jax.numpy as jnp
import numpy as np
from jax import lax
from jax.experimental import pallas as pl
from jax.experimental.pallas import tpu as pltpu
from jax.sharding import PartitionSpec as P

NB = 32
DIST = 128
EPSILON = 1e-06
NEGATIVE = -1e30
HIGHEST = lax.Precision.HIGHEST
F32 = jnp.float32
BF16 = jnp.bfloat16
BLK = 256
LANES = 128
VMEM_LIMIT = 56 * 1024 * 1024

NN = (((1,), (0,)), ((), ()))
NT = (((1,), (1,)), ((), ()))
TN = (((0,), (0,)), ((), ()))


def dot(a, b, dims=NN, precision=None):
    return lax.dot_general(a, b, dims, precision=precision, preferred_element_type=F32)


def bucket_of(distance):
    halfway = NB // 2
    thresholds = [
        int(math.ceil(halfway * (DIST / halfway) ** (step / halfway))) for step in range(halfway)
    ]
    beyond = sum((distance >= threshold).astype(np.int64) for threshold in thresholds)
    return np.where(distance < halfway, distance, halfway - 1 + beyond)


def near_tables():
    lanes = np.arange(2 * BLK)
    offset = np.where(lanes < BLK, lanes, lanes - 2 * BLK)
    build = np.stack([np.maximum(offset, 0), np.maximum(BLK + offset, 0)])
    gather = np.stack([lanes - (BLK - 1), lanes + 1])
    eye = np.eye(NB, dtype=np.float32)
    build_hot = eye[bucket_of(build)]
    gather_hot = eye[bucket_of(np.maximum(gather, 0))] * (gather >= 0)[..., None]
    return build_hot, gather_hot


def row_scale(values):
    return lax.rsqrt(jnp.mean(values * values, axis=-1, keepdims=True) + EPSILON)


def lane_pick(values, index):
    lanes = lax.broadcasted_iota(jnp.int32, values.shape, 1)
    return jnp.sum(jnp.where(lanes == index, values, 0.0), axis=1, keepdims=True)


def masked_scores(k_tile, qh_tile, bias, seg_k, seg_q, diagonal):
    scores = dot(k_tile, qh_tile, NT) + bias
    allowed = seg_k == seg_q
    if diagonal:
        key_at = lax.broadcasted_iota(jnp.int32, scores.shape, 0)
        query_at = lax.broadcasted_iota(jnp.int32, scores.shape, 1)
        allowed = allowed & (key_at <= query_at)
    return jnp.where(allowed, scores, NEGATIVE)


def tile_bias(bias_ref, far_ref, head, delta):
    if delta < 2:
        return bias_ref[2 * head + delta]
    return far_ref[pl.ds(head, 1), 0:1]


def attn_fwd_kernel(
    heads, head_size, tok, gain, w, seg_row, seg_col, near, far,
    normed, qh, k, v, att, ot, lse, bias, vt,
):
    rows_total = tok.shape[0]
    features = w.shape[2]
    blocks = rows_total // BLK
    gain_row = gain[...].astype(F32)
    lanes = lax.broadcasted_iota(jnp.int32, (BLK, features), 1)
    for block in range(blocks):
        rows = pl.ds(block * BLK, BLK)
        x = tok[rows, :].astype(F32)
        n = (x * row_scale(x) * gain_row).astype(BF16)
        normed[rows, :] = n
        q_rows = dot(n, w[0]).astype(BF16).astype(F32) * (head_size**-0.5)
        for head in range(heads):
            inside = (lanes >= head * head_size) & (lanes < (head + 1) * head_size)
            qh[head, rows, :] = jnp.where(inside, q_rows, 0.0).astype(BF16)
        k[rows, :] = dot(n, w[1]).astype(BF16)
        v_rows = dot(n, w[2]).astype(BF16)
        v[rows, :] = v_rows
        vt[:, rows] = v_rows.astype(F32).T.astype(BF16)
    for index in range(2 * heads):
        spread = jnp.broadcast_to(near[index : index + 1, :], (BLK, 2 * BLK))
        bias[index] = pltpu.roll(spread, 0, 1, stride=1, stride_axis=0)[:, :BLK]
    lse[...] = jnp.zeros_like(lse)

    def one_head(head, carry):
        part = pl.ds(pl.multiple_of(head * head_size, head_size), head_size)
        for qb in range(blocks):
            cols = pl.ds(qb * BLK, BLK)
            q_tile = qh[head, cols, :]
            tiles = []
            for kb in range(qb + 1):
                keys = pl.ds(kb * BLK, BLK)
                tiles.append(
                    masked_scores(
                        k[keys, :], q_tile, tile_bias(bias, far, head, qb - kb),
                        seg_col[keys, :], seg_row[:, cols], kb == qb,
                    )
                )
            peak = functools.reduce(
                jnp.maximum, [jnp.max(t, axis=0, keepdims=True) for t in tiles]
            )
            total = jnp.zeros((1, BLK), F32)
            out = jnp.zeros((head_size, BLK), F32)
            for kb in range(qb + 1):
                raised = jnp.exp(tiles[kb] - peak)
                total = total + jnp.sum(raised, axis=0, keepdims=True)
                out = out + dot(vt[part, kb * BLK : (kb + 1) * BLK], raised.astype(BF16))
            ot[part, cols] = out / total
            lse[pl.ds(head, 1), cols] = peak + jnp.log(total)
        return carry

    lax.fori_loop(0, heads, one_head, 0)
    for block in range(blocks):
        cols = pl.ds(block * BLK, BLK)
        att[cols, :] = ot[:, cols].T.astype(BF16)


def attn_bwd_kernel(heads, head_size, shares, idx, *refs):
    go_parts, refs = refs[:shares], refs[shares:]
    qh, k, v, ot, lse, bias, far, seg_row, seg_col, w = refs[:10]
    refs = refs[10:]
    gn_parts, refs = refs[:shares], refs[shares:]
    gproj, near_sum, far_sum, go, gq_t, gk, gv, kt, d_row, acc, acc_far = refs
    rows_total, features = k.shape
    blocks = rows_total // BLK
    share = rows_total // shares
    me = idx[0]
    for step in range(shares):
        start = pl.multiple_of(lax.rem(me + step, shares) * share, share)
        go[pl.ds(start, share), :] = go_parts[step][...]
    for block in range(blocks):
        cols = pl.ds(block * BLK, BLK)
        kt[:, cols] = k[cols, :].astype(F32).T.astype(BF16)
        product = go[cols, :].astype(F32).T * ot[:, cols]
        for head in range(heads):
            part = product[head * head_size : (head + 1) * head_size, :]
            d_row[head : head + 1, cols] = jnp.sum(part, axis=0, keepdims=True)
    gk[...] = jnp.zeros_like(gk)
    gv[...] = jnp.zeros_like(gv)
    near_sum[...] = jnp.zeros_like(near_sum)
    far_sum[...] = jnp.zeros_like(far_sum)
    key_at = lax.broadcasted_iota(jnp.int32, (BLK, BLK), 0)
    other_at = lax.broadcasted_iota(jnp.int32, (BLK, BLK), 1)
    flip = (key_at + other_at == BLK - 1).astype(F32)

    def one_head(head, carry):
        part = pl.ds(pl.multiple_of(head * head_size, head_size), head_size)
        lanes = lax.broadcasted_iota(jnp.int32, (BLK, features), 1)
        inside = (lanes >= head * head_size) & (lanes < (head + 1) * head_size)
        acc[...] = jnp.zeros_like(acc)
        acc_far[...] = jnp.zeros_like(acc_far)
        for qb in range(blocks):
            cols = pl.ds(qb * BLK, BLK)
            q_tile = qh[head, cols, :]
            go_tile = jnp.where(inside, go[cols, :].astype(F32), 0.0).astype(BF16)
            log_total = lse[pl.ds(head, 1), cols]
            d_tile = d_row[pl.ds(head, 1), cols]
            gq = jnp.zeros((head_size, BLK), F32)
            for kb in range(qb + 1):
                keys = pl.ds(kb * BLK, BLK)
                delta = qb - kb
                scores = masked_scores(
                    k[keys, :], q_tile, tile_bias(bias, far, head, delta),
                    seg_col[keys, :], seg_row[:, cols], delta == 0,
                )
                probs = jnp.exp(scores - log_total)
                gs = probs * (dot(v[keys, :], go_tile, NT) - d_tile)
                if delta < 2:
                    acc[delta] += gs
                else:
                    acc_far[...] += gs
                gs_low = gs.astype(BF16)
                gv[keys, :] += dot(probs.astype(BF16), go_tile)
                gk[keys, :] += dot(gs_low, q_tile)
                gq = gq + dot(kt[part, kb * BLK : (kb + 1) * BLK], gs_low)
            gq_t[part, cols] = gq * (head_size**-0.5)
        for delta in range(2):
            turned = dot(flip, acc[delta], NN, HIGHEST)
            wide = jnp.concatenate([turned, jnp.zeros_like(turned)], axis=1)
            sheared = pltpu.roll(wide, 0, 1, stride=1, stride_axis=0)
            near_sum[pl.ds(2 * head + delta, 1), :] = jnp.sum(sheared, axis=0, keepdims=True)
        far_sum[pl.ds(head, 1), :] = jnp.sum(acc_far[...], axis=0, keepdims=True)
        return carry

    lax.fori_loop(0, heads, one_head, 0)
    for block in range(blocks):
        rows = pl.ds(block * BLK, BLK)
        gproj[0, rows, :] = gq_t[:, rows].T.astype(BF16)
        gproj[1, rows, :] = gk[rows, :].astype(BF16)
        gproj[2, rows, :] = gv[rows, :].astype(BF16)
    for step in range(shares):
        start = pl.multiple_of(lax.rem(me + step, shares) * share, share)
        rows = pl.ds(start, share)
        total = dot(gproj[0, rows, :], w[0], NT)
        total = total + dot(gproj[1, rows, :], w[1], NT)
        total = total + dot(gproj[2, rows, :], w[2], NT)
        gn_parts[step][...] = total.astype(BF16)


def gelu_pair(values):
    inner = 0.7978845608028654 * (values + 0.044715 * values * values * values)
    bent = jnp.tanh(inner)
    half = 0.5 * (1.0 + bent)
    slope = 0.7978845608028654 * (1.0 + 3.0 * 0.044715 * values * values)
    return values * half, half + 0.5 * values * (1.0 - bent * bent) * slope


ROWS = 512


def moe_fwd_kernel(shares, experts, idx, *refs):
    att, refs = refs[:shares], refs[shares:]
    wo, refs = refs[:shares], refs[shares:]
    tok, gain, router, routes, cot, w_in, w_down = refs[:7]
    refs = refs[7:]
    parts, refs = refs[:shares], refs[shares:]
    normed, own, gates, ggate, act, slope, acc = refs
    rows_total = tok.shape[0]
    share = rows_total // shares
    me = idx[0]
    expert = pl.program_id(0)

    @pl.when(expert == 0)
    def _():
        gain_row = gain[...].astype(F32)
        for block in range(rows_total // BLK):
            rows = pl.ds(block * BLK, BLK)
            hidden = tok[rows, :].astype(F32)
            attn = dot(att[0][rows, :], wo[0][...])
            for step in range(1, shares):
                attn = attn + dot(att[step][rows, :], wo[step][...])
            hidden = hidden + attn
            acc[rows, :] = hidden
            n = (hidden * row_scale(hidden) * gain_row).astype(BF16)
            normed[rows, :] = n
            logits = dot(n, router[...])
            lanes = lax.broadcasted_iota(jnp.int32, logits.shape, 1)
            first = lanes == routes[rows, 0:1]
            second = lanes == routes[rows, 1:2]
            one = jnp.sum(jnp.where(first, logits, 0.0), axis=1, keepdims=True)
            two = jnp.sum(jnp.where(second, logits, 0.0), axis=1, keepdims=True)
            peak = jnp.maximum(one, two)
            one = jnp.exp(one - peak)
            two = jnp.exp(two - peak)
            both = one + two
            gates[rows, :] = jnp.where(first, one / both, jnp.where(second, two / both, 0.0))
        own[...] = acc[pl.ds(pl.multiple_of(me * share, share), share), :]
        acc[...] = jnp.zeros_like(acc)
        ggate[...] = jnp.zeros_like(ggate)

    for block in range(rows_total // ROWS):
        rows = pl.ds(block * ROWS, ROWS)
        lifted, bend = gelu_pair(dot(normed[rows, :], w_in[0]))
        lifted = lifted.astype(BF16)
        act[0, rows, :] = lifted
        slope[0, rows, :] = bend.astype(BF16)
        out = dot(lifted, w_down[0])
        gate = lane_pick(gates[rows, :], expert)
        acc[rows, :] += gate * out
        pulled = jnp.sum(cot[rows, :].astype(F32) * out, axis=1, keepdims=True)
        held = ggate[rows, :]
        lanes = lax.broadcasted_iota(jnp.int32, held.shape, 1)
        ggate[rows, :] = jnp.where(lanes == expert, pulled, held)

    @pl.when(expert == experts - 1)
    def _():
        for step in range(shares):
            start = pl.multiple_of(lax.rem(me + step, shares) * share, share)
            parts[step][...] = acc[pl.ds(start, share), :].astype(BF16)


def moe_bwd_kernel(shares, experts, idx, *refs):
    gates, ggate, cot, slope, router_t, w_in, w_down = refs[:7]
    refs = refs[7:]
    parts, refs = refs[:shares], refs[shares:]
    glog, gpre, acc = refs
    rows_total = cot.shape[0]
    share = rows_total // shares
    me = idx[0]
    expert = pl.program_id(0)

    @pl.when(expert == 0)
    def _():
        for block in range(rows_total // ROWS):
            rows = pl.ds(block * ROWS, ROWS)
            g, gg = gates[rows, :], ggate[rows, :]
            back = g * (gg - jnp.sum(g * gg, axis=1, keepdims=True))
            glog[rows, :] = back
            acc[rows, :] = dot(back, router_t[...], NN, HIGHEST)

    for block in range(rows_total // ROWS):
        rows = pl.ds(block * ROWS, ROWS)
        gate = lane_pick(gates[rows, :], expert)
        weighted = (gate * cot[rows, :].astype(F32)).astype(BF16)
        gp = (dot(weighted, w_down[0], NT) * slope[0, rows, :].astype(F32)).astype(BF16)
        gpre[0, rows, :] = gp
        acc[rows, :] += dot(gp, w_in[0], NT)

    @pl.when(expert == experts - 1)
    def _():
        for step in range(shares):
            start = pl.multiple_of(lax.rem(me + step, shares) * share, share)
            parts[step][...] = acc[pl.ds(start, share), :].astype(BF16)


def moe_weights_kernel(gates, cot, normed, act, gpre, out):
    expert = pl.program_id(0)
    gate = lane_pick(gates[...], expert)
    weighted = (gate * cot[...].astype(F32)).astype(BF16)
    out[0, 0] = dot(normed[...], gpre[0], TN).astype(BF16)
    out[0, 1] = dot(act[0], weighted, TN).astype(BF16)


def hidden_back_kernel(shares, idx, *refs):
    gx, refs = refs[:shares], refs[shares:]
    wo, refs = refs[:shares], refs[shares:]
    own, cot, gain = refs[:3]
    refs = refs[3:]
    ga, refs = refs[:shares], refs[shares:]
    gh, gh_low, ggain = refs
    share = own.shape[0]
    grad = gx[0][...].astype(F32)
    for step in range(1, shares):
        grad = grad + gx[step][...].astype(F32)
    hidden = own[...]
    scale = row_scale(hidden)
    unit = hidden * scale
    ggain[...] = jnp.sum(grad * unit, axis=0, keepdims=True)
    gained = grad * gain[...].astype(F32)
    mine = cot[pl.ds(pl.multiple_of(idx[0] * share, share), share), :].astype(F32)
    back = mine + scale * (gained - unit * jnp.mean(gained * unit, axis=-1, keepdims=True))
    gh[...] = back
    low = back.astype(BF16)
    gh_low[...] = low
    for step in range(shares):
        ga[step][...] = dot(low, wo[step][...], NT).astype(BF16)


def w_out_back_kernel(shares, idx, *refs):
    att = refs[:shares]
    gh_low, out = refs[shares:]
    share = gh_low.shape[0]
    rows = pl.ds(pl.multiple_of(idx[0] * share, share), share)
    low = gh_low[...]
    for step in range(shares):
        out[step] = dot(att[step][rows, :], low, TN).astype(BF16)


def input_back_kernel(shares, idx, *refs):
    gn, refs = refs[:shares], refs[shares:]
    tok, gh, gain, gt, ggain = refs
    share = gh.shape[0]
    grad = gn[0][...].astype(F32)
    for step in range(1, shares):
        grad = grad + gn[step][...].astype(F32)
    x = tok[pl.ds(pl.multiple_of(idx[0] * share, share), share), :].astype(F32)
    scale = row_scale(x)
    unit = x * scale
    ggain[...] = jnp.sum(grad * unit, axis=0, keepdims=True)
    gained = grad * gain[...].astype(F32)
    back = gh[...] + scale * (gained - unit * jnp.mean(gained * unit, axis=-1, keepdims=True))
    gt[...] = back.astype(BF16)


def place_kernel(shares, idx, *refs):
    blocks, out = refs[:shares], refs[shares]
    share = out.shape[0] // shares
    for step in range(shares):
        start = pl.multiple_of(lax.rem(idx[0] + shares - step, shares) * share, share)
        out[pl.ds(start, share), :] = blocks[step][...].astype(out.dtype)


SMEM = pl.BlockSpec(memory_space=pltpu.SMEM)
VMEM = pl.BlockSpec(memory_space=pltpu.VMEM)


def shaped(shape, dtype):
    return jax.ShapeDtypeStruct(shape, dtype)


def whole_call(kernel, outs, args, scratch=(), flops=0, moved=0, with_index=True):
    specs = ([SMEM] if with_index else []) + [VMEM] * (len(args) - (1 if with_index else 0))
    return pl.pallas_call(
        kernel,
        out_shape=outs,
        in_specs=specs,
        out_specs=[VMEM] * len(outs),
        scratch_shapes=list(scratch),
        compiler_params=pltpu.CompilerParams(vmem_limit_bytes=VMEM_LIMIT),
        cost_estimate=pl.CostEstimate(flops=flops, bytes_accessed=moved, transcendentals=0),
    )(*args)


def shift(value, axis, by):
    count = lax.axis_size(axis)
    return lax.ppermute(value, axis, [(i, (i + by) % count) for i in range(count)])


def swap(value, axis, bit):
    count = lax.axis_size(axis)
    return lax.ppermute(value, axis, [(i, i ^ bit) for i in range(count)])


def sum_over(value, axis):
    bit = 1
    while bit < lax.axis_size(axis):
        value = value + swap(value, axis, bit)
        bit *= 2
    return value


def body(
    tokens, segments, routes, grad_out, gain_attn, w_qkv, w_out, rel_bias,
    gain_moe, w_router, w_in, w_down,
):
    tok_rows, width = tokens.shape
    heads = rel_bias.shape[1]
    features = w_qkv.shape[2]
    head_size = features // heads
    experts, _, hidden_units = w_in.shape
    shares = lax.axis_size("tensor")
    share = tok_rows // shares
    me = lax.axis_index("tensor").astype(jnp.int32)
    idx = me.reshape(1)
    mib = 1 << 20

    half_rows = features // 2
    side = lax.axis_index("dp") % 2
    my_half = lax.dynamic_slice_in_dim(w_out, side * half_rows, half_rows, 0)
    halves = jnp.stack([shift(my_half, "tensor", by) for by in range(1, shares)])
    others = swap(halves, "dp", 1)
    low_half = jnp.where(side == 0, halves, others)
    high_half = jnp.where(side == 0, others, halves)
    fetched = jnp.concatenate([low_half, high_half], axis=1)
    wo = [w_out] + [fetched[by] for by in range(shares - 1)]

    build_hot, gather_hot = near_tables()
    near = jnp.einsum(
        "dlb,bh->hdl", jnp.asarray(build_hot, BF16), rel_bias, preferred_element_type=F32
    ).reshape(2 * heads, 2 * BLK)
    near = jnp.pad(near, ((0, 8 - 2 * heads), (0, 0)))
    far = jnp.broadcast_to(rel_bias[NB - 1].astype(F32)[:, None], (heads, LANES))
    far = jnp.pad(far, ((0, 8 - heads), (0, 0)))
    seg_row = segments.reshape(1, tok_rows)
    seg_col = segments.reshape(tok_rows, 1)
    gain_one = gain_attn.reshape(1, width)
    gain_two = gain_moe.reshape(1, width)

    normed_one, qh, k, v, att, ot, lse, bias = whole_call(
        functools.partial(attn_fwd_kernel, heads, head_size),
        [
            shaped((tok_rows, width), BF16),
            shaped((heads, tok_rows, features), BF16),
            shaped((tok_rows, features), BF16),
            shaped((tok_rows, features), BF16),
            shaped((tok_rows, features), BF16),
            shaped((features, tok_rows), F32),
            shaped((8, tok_rows), F32),
            shaped((2 * heads, BLK, BLK), F32),
        ],
        [tokens, gain_one, w_qkv, seg_row, seg_col, near, far],
        [pltpu.VMEM((features, tok_rows), BF16)],
        flops=6 * 10**9, moved=8 * mib, with_index=False,
    )
    atts = [att] + [shift(att, "tensor", by) for by in range(1, shares)]

    router_wide = jnp.pad(w_router, ((0, 0), (0, LANES - experts)))
    full = lambda shape: pl.BlockSpec(shape, lambda e: (0,) * len(shape))
    per_expert = lambda shape: pl.BlockSpec((1,) + shape, lambda e: (e, 0, 0))
    params = pltpu.CompilerParams(
        vmem_limit_bytes=VMEM_LIMIT, dimension_semantics=("arbitrary",)
    )
    moe_flops = 4 * experts * tok_rows * width * hidden_units
    fwd = pl.pallas_call(
        functools.partial(moe_fwd_kernel, shares, experts),
        grid=(experts,),
        in_specs=[SMEM]
        + [full((tok_rows, features))] * shares
        + [full((features, width))] * shares
        + [
            full((tok_rows, width)), full((1, width)), full((width, LANES)),
            full((tok_rows, 2)), full((tok_rows, width)),
            per_expert((width, hidden_units)), per_expert((hidden_units, width)),
        ],
        out_specs=[full((share, width))] * shares
        + [
            full((tok_rows, width)), full((share, width)), full((tok_rows, LANES)),
            full((tok_rows, LANES)), per_expert((tok_rows, hidden_units)),
            per_expert((tok_rows, hidden_units)),
        ],
        out_shape=[shaped((share, width), BF16)] * shares
        + [
            shaped((tok_rows, width), BF16),
            shaped((share, width), F32),
            shaped((tok_rows, LANES), F32),
            shaped((tok_rows, LANES), F32),
            shaped((experts, tok_rows, hidden_units), BF16),
            shaped((experts, tok_rows, hidden_units), BF16),
        ],
        scratch_shapes=[pltpu.VMEM((tok_rows, width), F32)],
        compiler_params=params,
        cost_estimate=pl.CostEstimate(
            flops=moe_flops, bytes_accessed=32 * mib, transcendentals=0
        ),
    )(idx, *atts, *wo, tokens, gain_two, router_wide, routes, grad_out, w_in, w_down)
    moe_parts = fwd[:shares]
    normed_two, own_hidden, gates, ggate, act, slope = fwd[shares:]

    moe_got = [moe_parts[0]] + [shift(moe_parts[by], "tensor", by) for by in range(1, shares)]

    router_t = jnp.pad(w_router.astype(F32).T, ((0, LANES - experts), (0, 0)))
    bwd = pl.pallas_call(
        functools.partial(moe_bwd_kernel, shares, experts),
        grid=(experts,),
        in_specs=[
            SMEM, full((tok_rows, LANES)), full((tok_rows, LANES)), full((tok_rows, width)),
            per_expert((tok_rows, hidden_units)), full((LANES, width)),
            per_expert((width, hidden_units)), per_expert((hidden_units, width)),
        ],
        out_specs=[full((share, width))] * shares
        + [full((tok_rows, LANES)), per_expert((tok_rows, hidden_units))],
        out_shape=[shaped((share, width), BF16)] * shares
        + [
            shaped((tok_rows, LANES), F32),
            shaped((experts, tok_rows, hidden_units), BF16),
        ],
        scratch_shapes=[pltpu.VMEM((tok_rows, width), F32)],
        compiler_params=params,
        cost_estimate=pl.CostEstimate(
            flops=moe_flops, bytes_accessed=26 * mib, transcendentals=0
        ),
    )(idx, gates, ggate, grad_out, slope, router_t, w_in, w_down)
    gx_parts = bwd[:shares]
    glog, gpre = bwd[shares:]
    gx_got = [gx_parts[0]] + [shift(gx_parts[by], "tensor", by) for by in range(1, shares)]

    expert_grads = pl.pallas_call(
        moe_weights_kernel,
        grid=(experts,),
        in_specs=[
            full((tok_rows, LANES)), full((tok_rows, width)), full((tok_rows, width)),
            per_expert((tok_rows, hidden_units)), per_expert((tok_rows, hidden_units)),
        ],
        out_specs=[pl.BlockSpec((1, 2, width, width), lambda e: (e, 0, 0, 0))],
        out_shape=[shaped((experts, 2, width, width), BF16)],
        compiler_params=params,
        cost_estimate=pl.CostEstimate(
            flops=moe_flops, bytes_accessed=26 * mib, transcendentals=0
        ),
    )(gates, grad_out, normed_two, act, gpre)[0]
    expert_rows = expert_grads.reshape(experts * 2 * width, width)
    expert_rows = lax.psum_scatter(expert_rows, "dp", scatter_dimension=0, tiled=True)
    expert_rows = lax.all_gather(expert_rows, "dp", axis=0, tiled=True)
    expert_rows = expert_rows.reshape(experts, 2, width, width)
    grad_w_in = expert_rows[:, 0].astype(F32)
    grad_w_down = expert_rows[:, 1].astype(F32)

    grad_router = jnp.dot(glog[:, :experts].T, normed_two.astype(F32), precision=HIGHEST)

    back = whole_call(
        functools.partial(hidden_back_kernel, shares),
        [shaped((share, features), BF16)] * shares
        + [shaped((share, width), F32), shaped((share, width), BF16), shaped((1, width), F32)],
        [idx, *gx_got, *wo, own_hidden, grad_out, gain_two],
        flops=3 * 10**8, moved=6 * mib,
    )
    ga_parts = back[:shares]
    grad_hidden, grad_hidden_low, ggain_two = back[shares:]
    ga_got = [ga_parts[0]] + [shift(ga_parts[by], "tensor", -by) for by in range(1, shares)]
    w_out_rows = whole_call(
        functools.partial(w_out_back_kernel, shares),
        [shaped((shares, features, width), BF16)],
        [idx, *atts, grad_hidden_low],
        flops=3 * 10**8, moved=4 * mib,
    )[0]

    result_share = own_hidden
    for piece in moe_got:
        result_share = result_share + piece.astype(F32)
    result_share = result_share.astype(BF16)
    result_got = [result_share] + [shift(result_share, "tensor", by) for by in range(1, shares)]
    result = whole_call(
        functools.partial(place_kernel, shares),
        [shaped((tok_rows, width), BF16)], [idx, *result_got], moved=3 * mib,
    )[0]

    attn_back = whole_call(
        functools.partial(attn_bwd_kernel, heads, head_size, shares),
        [shaped((share, width), BF16)] * shares
        + [
            shaped((3, tok_rows, features), BF16),
            shaped((8, 2 * BLK), F32),
            shaped((8, BLK), F32),
        ],
        [idx, *ga_got, qh, k, v, ot, lse, bias, far, seg_row, seg_col, w_qkv],
        [
            pltpu.VMEM((tok_rows, features), BF16),
            pltpu.VMEM((features, tok_rows), F32),
            pltpu.VMEM((tok_rows, features), F32),
            pltpu.VMEM((tok_rows, features), F32),
            pltpu.VMEM((features, tok_rows), BF16),
            pltpu.VMEM((8, tok_rows), F32),
            pltpu.VMEM((2, BLK, BLK), F32),
            pltpu.VMEM((BLK, BLK), F32),
        ],
        flops=14 * 10**9, moved=8 * mib,
    )
    gn_parts = attn_back[:shares]
    gproj, near_sum, far_sum = attn_back[shares:]
    gn_got = [gn_parts[0]] + [shift(gn_parts[by], "tensor", by) for by in range(1, shares)]

    qkv_rows = jnp.einsum("ctf,td->cfd", gproj, normed_one, preferred_element_type=F32)
    late_rows = jnp.concatenate(
        [
            qkv_rows.astype(BF16).reshape(3 * features, width),
            w_out_rows.reshape(shares * features, width),
        ],
        axis=0,
    )
    late_rows = lax.psum_scatter(late_rows, "dp", scatter_dimension=1, tiled=True)
    late_qkv = late_rows[: 3 * features]
    late_out = late_rows[3 * features :].reshape(shares, features, -1)
    out_sum = late_out[0].astype(F32)
    for by in range(1, shares):
        out_sum = out_sum + shift(late_out[by], "tensor", -by).astype(F32)
    late_rows = jnp.concatenate([late_qkv, out_sum.astype(BF16)], axis=0)
    late_rows = lax.all_gather(late_rows, "dp", axis=1, tiled=True)
    grad_w_qkv = late_rows[: 3 * features].reshape(3, features, width)
    grad_w_qkv = jnp.swapaxes(grad_w_qkv, 1, 2).astype(F32)
    grad_w_out = late_rows[3 * features :].astype(F32)

    gt_share, ggain_one = whole_call(
        functools.partial(input_back_kernel, shares),
        [shaped((share, width), BF16), shaped((1, width), F32)],
        [idx, *gn_got, tokens, grad_hidden, gain_one],
        moved=5 * mib,
    )
    gt_got = [gt_share] + [shift(gt_share, "tensor", by) for by in range(1, shares)]
    grad_tokens = whole_call(
        functools.partial(place_kernel, shares),
        [shaped((tok_rows, width), F32)], [idx, *gt_got], moved=5 * mib,
    )[0]

    near_part = jnp.einsum(
        "hdl,dlb->bh",
        near_sum[: 2 * heads].reshape(heads, 2, 2 * BLK),
        jnp.asarray(gather_hot, F32),
        precision=HIGHEST,
    )
    far_part = jnp.sum(far_sum[:heads], axis=1)
    grad_rel = near_part.at[NB - 1].add(far_part)
    rel_row = jnp.pad(grad_rel.reshape(1, -1), ((0, 0), (0, width - NB * heads)))
    small = jnp.concatenate([rel_row, ggain_one, ggain_two, grad_router], axis=0)
    small = sum_over(small, "dp")
    grad_rel_bias = small[0, : NB * heads].reshape(NB, heads)
    shared = sum_over(small[1:], "tensor")
    return (
        result,
        grad_tokens,
        shared[0],
        grad_w_qkv,
        grad_w_out,
        grad_rel_bias,
        shared[1],
        shared[2:].T,
        grad_w_in,
        grad_w_down,
    )


def solution(mesh):
    placed = (
        P("dp", None),
        P("dp", None),
        P("dp", None),
        P("dp", None),
        P(),
        P(None, None, "tensor"),
        P("tensor", None),
        P(None, "tensor"),
        P(),
        P(),
        P(None, None, "tensor"),
        P(None, "tensor", None),
    )
    return jax.shard_map(
        body,
        mesh=mesh,
        in_specs=placed,
        out_specs=(
            P("dp", None),
            P("dp", None),
            P(),
            P(None, None, "tensor"),
            P("tensor", None),
            P(None, "tensor"),
            P(),
            P(),
            P(None, None, "tensor"),
            P(None, "tensor", None),
        ),
        check_vma=False,
    )
```

time: 1200 us -> 529 us (0.44); the launches traced: 1180 us -> 529 us
  waiting for transfers between devices: 547 us -> 278 us
  matrix products: 258 us -> 4.66 us
  local copies, waits for them, and re-layouts: 207 us -> 28.1 us
  Pallas kernels: 0 us -> 108 us
  starting transfers between devices: 0.67 us -> 78.3 us
  other arithmetic: 95.1 us -> 17.8 us
  blocking collectives: 47.2 us -> 0 us
  loops' own time: 14.6 us -> 0 us
    dot_general x33 -> x4, matrix products: 252 us -> 4.66 us  [the longest x1 2.71 us: body(): jnp.einsum('ctf,td->cfd', gproj, normed_one, preferred_element_type=F32)]
    psum x3 -> x0, waiting for transfers between devices: 184 us -> none  [the longest x1 98 us: body(): attn_sum = lax.psum(attn_part, 'tensor')]
    ppermute x0 -> x33, waiting for transfers between devices: none -> 183 us  [the longest x27 147 us: shift(): lax.ppermute(value, axis, [(i, (i + by) % count) for i in range(count)])]
    pallas_call x0 -> x10, Pallas kernels: none -> 108 us  [the longest x7 45.1 us: whole_call(): pl.pallas_call(kernel, out_shape=outs, in_specs=specs, out_specs=[VMEM] *...]
    reduce_scatter x3 -> x1, waiting for transfers between devices: 176 us -> 70.2 us  [body(): lax.psum_scatter(expert_rows, 'dp', scatter_dimension=0, tiled=True)]
    all_gather x3 -> x2, waiting for transfers between devices: 87.3 us -> 0.01 us  [the longest x1 0.01 us: body(): late_rows = lax.all_gather(late_rows, 'dp', axis=1, tiled=True)]
    ppermute x0 -> x33, starting transfers between devices: none -> 78.1 us  [the longest x27 58.7 us: shift(): lax.ppermute(value, axis, [(i, (i + by) % count) for i in range(count)])]
    unnamed x15 -> x5, waiting for transfers between devices: 99.6 us -> 24.8 us
  transfers between devices with their start and end apart: 12 -> 37, of which waited for: 12 -> 18; matrix products, arithmetic and copies ran while one was open for 13% -> 5% of each run, Pallas kernels for 0% -> 7%
where the time goes in v1:
time: 529 us
  waiting for transfers between devices  278 us (53%)
  Pallas kernels  108 us (20%)
  starting transfers between devices  78.3 us (15%)
  local copies, waits for them, and re-layouts  28.1 us (5%)
  other arithmetic  17.8 us (3%)
  between operations  14.2 us (3%)
    ppermute x27, waiting for transfers between devices, shift(): lax.ppermute(value, axis, [(i, (i + by) % count) for i in range(count)])  147 us
    reduce_scatter x1, waiting for transfers between devices, body(): lax.psum_scatter(expert_rows, 'dp', scatter_dimension=0, tiled=True)  70.2 us
    ppermute x27, starting transfers between devices, shift(): lax.ppermute(value, axis, [(i, (i + by) % count) for i in range(count)])  58.7 us
    pallas_call x7, Pallas kernels, whole_call(): pl.pallas_call(kernel, out_shape=outs, in_specs=specs, out_specs=[VMEM] *...  45.1 us
    ppermute x6, waiting for transfers between devices, swap(): return lax.ppermute(value, axis, [(i, i ^ bit) for i in range(count)])  35.5 us
    pallas_call x1, Pallas kernels, body(): pl.pallas_call(functools.partial(moe_fwd_kernel, shares, experts), grid=(...  27.4 us
    unnamed x5, waiting for transfers between devices  24.8 us
    pallas_call x1, Pallas kernels, body(): pl.pallas_call(functools.partial(moe_bwd_kernel, shares, experts), grid=(...  19.7 us
  transfers between devices with their start and end apart: 37, of which 18 were waited for; matrix products, arithmetic and copies ran while one was open for 5% of the time, Pallas kernels for 7%

profile of v1, /device:TPU:0, one launch (start us, length us, event | category | flops | bytes accessed | tf_op | source)
XLA Modules:
  0.0 528.6 jit_solution(17910641655997618758)
XLA Ops:
  8.2 5.1 collective-permute-start.5
  21.4 4.3 collective-permute-done.4
  26.6 11.7 %shard_map.213 = (bf16[1024,768]{1,0:T(8,128)(2,1)}, bf16[3,1024,192]{2,1,0:T(8,128)(2,1)}, bf16[1024,192]{1,0:T(8,128)(2,1)}, bf16[1024,192]{1,0:T(8,128)(2,1)}...) custom-call(bf16[1024,768]{1,0:T(8,128)(2,1)} %refs_4_.5, ...), custom_call_target="tpu_custom_call" | custom-call | flops 6000000000 | bytes 8388608 | tf_op jit(solution)/shard_map/pallas_call | solution.py:402
  41.1 2.9 collective-permute-start.2
  48.3 6.8 %collective-permute-done.refs_1_ = bf16[1024,192]{1,0:T(8,128)(2,1)S(1)} collective-permute-done((bf16[1024,192]{1,0:T(8,128)(2,1)}, bf16[1024,192]{1,0:T(8,128)(2,1)S(1)}, u32[]{:S(2)}, u32[]{:S(2)}) %collective-permute-start) | collective-permute-done | bytes 393248 | tf_op jit(solution)/shard_map/ppermute | solution.py:415
  55.1 22.0 %collective-permute-done.1.refs_2_ = bf16[1024,192]{1,0:T(8,128)(2,1)S(1)} collective-permute-done((bf16[1024,192]{1,0:T(8,128)(2,1)}, bf16[1024,192]{1,0:T(8,128)(2,1)S(1)}, u32[]{:S(2)}, u32[]{:S(2)}) %collective-permute-start.1) | collective-permute-done | bytes 393248 | tf_op jit(solution)/shard_map/ppermute | solution.py:415
  78.2 27.4 %shard_map.214 = (bf16[256,768]{1,0:T(8,128)(2,1)}, bf16[256,768]{1,0:T(8,128)(2,1)}, bf16[256,768]{1,0:T(8,128)(2,1)}, bf16[256,768]{1,0:T(8,128)(2,1)}, bf16[1...) custom-call(s32[1]{0:T(128)} %bitcast.idx, ...), custom_call_target="tpu_custom_call" | custom-call | flops 9663676416 | bytes 33554432 | tf_op jit(solution)/shard_map/pallas_call | solution.py:493
  105.6 19.7 %shard_map.216 = (bf16[256,768]{1,0:T(8,128)(2,1)}, bf16[256,768]{1,0:T(8,128)(2,1)}, bf16[256,768]{1,0:T(8,128)(2,1)}, bf16[256,768]{1,0:T(8,128)(2,1)}, f32[10...) custom-call(s32[1]{0:T(128)} %bitcast.idx, f32[1024,128]{1,0:T(8,128)} %get-tuple-element.68.refs_0_.gates, ...), custom_call_target="tpu_custom_call" | custom-call | flops 9663676416 | bytes 27262976 | tf_op jit(solution)/shard_map/pallas_call | solution.py:531
  125.3 11.3 %collective-permute-start.13 = (bf16[256,768]{1,0:T(8,128)(2,1)}, bf16[256,768]{1,0:T(8,128)(2,1)S(1)}, u32[]{:S(2)}, u32[]{:S(2)}) collective-permute-start(bf16[256,768]{1,0:T(8,128)(2,1)} %get-tuple-element.72), channel_id=1, source_target_pairs={{0,1},{1,2},{2,3},{3,0},{4,5},{5,6},{6,7},{7,4},{8,9},{9,10},{10,1... | collective-permute-start | bytes 1179656 | tf_op jit(solution)/shard_map/ppermute | solution.py:415
  139.0 9.7 %collective-permute-done.13.refs_1_ = bf16[256,768]{1,0:T(8,128)(2,1)S(1)} collective-permute-done((bf16[256,768]{1,0:T(8,128)(2,1)}, bf16[256,768]{1,0:T(8,128)(2,1)S(1)}, u32[]{:S(2)}, u32[]{:S(2)}) %collective-permute-start.13) | collective-permute-done | bytes 393248 | tf_op jit(solution)/shard_map/ppermute | solution.py:415
  148.6 15.9 %collective-permute-done.14.refs_2_ = bf16[256,768]{1,0:T(8,128)(2,1)S(1)} collective-permute-done((bf16[256,768]{1,0:T(8,128)(2,1)}, bf16[256,768]{1,0:T(8,128)(2,1)S(1)}, u32[]{:S(2)}, u32[]{:S(2)}) %collective-permute-start.14) | collective-permute-done | bytes 393248 | tf_op jit(solution)/shard_map/ppermute | solution.py:415
  165.4 4.5 shard_map.217
  169.9 8.9 %collective-permute-start.16 = (bf16[256,192]{1,0:T(8,128)(2,1)}, bf16[256,192]{1,0:T(8,128)(2,1)S(1)}, u32[]{:S(2)}, u32[]{:S(2)}) collective-permute-start(bf16[256,192]{1,0:T(8,128)(2,1)} %get-tuple-element.76), channel_id=1, source_target_pairs={{0,3},{1,0},{2,1},{3,2},{4,7},{5,4},{6,5},{7,6},{8,11},{9,8},{10,9... | collective-permute-start | bytes 294920 | tf_op jit(solution)/shard_map/ppermute | solution.py:415
  180.1 3.2 shard_map.221
  183.3 8.8 %collective-permute-done.17.refs_2_ = bf16[256,192]{1,0:T(8,128)(2,1)S(1)} collective-permute-done((bf16[256,192]{1,0:T(8,128)(2,1)}, bf16[256,192]{1,0:T(8,128)(2,1)S(1)}, u32[]{:S(2)}, u32[]{:S(2)}) %collective-permute-start.17) | collective-permute-done | bytes 98336 | tf_op jit(solution)/shard_map/ppermute | solution.py:415
  192.9 16.5 %shard_map.218 = (bf16[256,768]{1,0:T(8,128)(2,1)}, bf16[256,768]{1,0:T(8,128)(2,1)}, bf16[256,768]{1,0:T(8,128)(2,1)}, bf16[256,768]{1,0:T(8,128)(2,1)}, bf16[3...) custom-call(s32[1]{0:T(128)} %bitcast.idx, bf16[256,192]{1,0:T(8,128)(2,1)} %get-tuple-element.75.refs_0_, ...), custom_call_target="tpu_custom_call" | custom-call | flops 14000000000 | bytes 8388608 | tf_op jit(solution)/shard_map/pallas_call | solution.py:402
  209.3 2.7 fusion.4
  214.7 15.3 %shard_map.222 = bf16[4,2,768,768]{3,2,1,0:T(8,128)(2,1)} custom-call(f32[1024,128]{1,0:T(8,128)} %get-tuple-element.68.refs_0_.gates, bf16[1024,768]{1,0:T(8,128)(2,1)} %cot.1, bf16[1024,768]{1,0:T(8,128)(2,1)} %get-tuple-element.96.normed, bf16[4,1024,768]{2,1,0:T(8,128)(2,1)} %get-tuple-element.100.act, bf16[4,1024,768]{2,1,0:T(8,128)(2,1)} %get-tuple-element.101.gpre), custom_call_target="tpu_custom_call" | custom-call | flops 9663676416 | bytes 27262976 | tf_op jit(solution)/shard_map/pallas_call | solution.py:556
  230.0 24.7 %reduce-scatter.7.cloned.1.call-done = bf16[96,1344]{1,0:T(8,128)(2,1)} async-done(((bf16[768,1344]{1,0:T(8,128)(2,1)}), bf16[96,1344]{1,0:T(8,128)(2,1)}) %reduce-scatter.7.cloned.1.call-update) | async-done | bytes 258064
  265.5 70.2 %reduce-scatter.5.cloned.1.call-done = bf16[768,768]{1,0:T(8,128)(2,1)} async-done(((bf16[6144,768]{1,0:T(8,128)(2,1)}), bf16[768,768]{1,0:T(8,128)(2,1)}) %reduce-scatter.5.cloned.1.call-update) | async-done | bytes 1179664 | tf_op jit(solution)/shard_map/reduce_scatter | solution.py:571
  335.8 3.4 collective-permute-start.9
  341.1 7.9 %collective-permute-done.9 = bf16[256,768]{1,0:T(8,128)(2,1)S(1)} collective-permute-done((bf16[256,768]{1,0:T(8,128)(2,1)}, bf16[256,768]{1,0:T(8,128)(2,1)S(1)}, u32[]{:S(2)}, u32[]{:S(2)}) %collective-permute-start.9) | collective-permute-done | bytes 393248 | tf_op jit(solution)/shard_map/ppermute | solution.py:415
  349.0 24.1 %collective-permute-done.8 = bf16[256,768]{1,0:T(8,128)(2,1)S(1)} collective-permute-done((bf16[256,768]{1,0:T(8,128)(2,1)}, bf16[256,768]{1,0:T(8,128)(2,1)S(1)}, u32[]{:S(2)}, u32[]{:S(2)}) %collective-permute-start.8) | collective-permute-done | bytes 393248 | tf_op jit(solution)/shard_map/ppermute | solution.py:415
  381.0 23.2 %collective-permute-done.19.refs_1_ = bf16[256,768]{1,0:T(8,128)(2,1)S(1)} collective-permute-done((bf16[256,768]{1,0:T(8,128)(2,1)}, bf16[256,768]{1,0:T(8,128)(2,1)S(1)}, u32[]{:S(2)}, u32[]{:S(2)}) %collective-permute-start.19) | collective-permute-done | bytes 393248 | tf_op jit(solution)/shard_map/ppermute | solution.py:415
  404.2 23.2 %collective-permute-done.20.refs_2_ = bf16[256,768]{1,0:T(8,128)(2,1)S(1)} collective-permute-done((bf16[256,768]{1,0:T(8,128)(2,1)}, bf16[256,768]{1,0:T(8,128)(2,1)S(1)}, u32[]{:S(2)}, u32[]{:S(2)}) %collective-permute-start.20) | collective-permute-done | bytes 393248 | tf_op jit(solution)/shard_map/ppermute | solution.py:415
  428.3 3.4 shard_map.219
  442.2 16.3 %collective-permute-start.28 = (f32[6,768]{1,0:T(8,128)S(1)}, f32[6,768]{1,0:T(8,128)S(1)}, u32[]{:S(2)}, u32[]{:S(2)}) collective-permute-start(f32[6,768]{1,0:T(8,128)S(1)} %slice.115), channel_id=1, source_target_pairs={{0,1},{1,0},{2,3},{3,2},{4,5},{5,4},{6,7},{7,6},{8,9},{9,8},{10,11... | collective-permute-start | bytes 55304 | tf_op jit(solution)/shard_map/ppermute | solution.py:420
  462.7 3.3 collective-permute-start.23
  466.0 2.9 collective-permute-start.24
  469.8 29.5 %collective-permute-done.29 = f32[6,768]{1,0:T(8,128)S(1)} collective-permute-done((f32[6,768]{1,0:T(8,128)S(1)}, f32[6,768]{1,0:T(8,128)S(1)}, u32[]{:S(2)}, u32[]{:S(2)}) %collective-permute-start.29) | collective-permute-done | bytes 18464 | tf_op jit(solution)/shard_map/ppermute | solution.py:420
  502.1 3.2 shard_map.220
  509.8 12.3 %fusion = (f32[4,768,768]{2,1,0:T(8,128)}, f32[4,768,768]{2,1,0:T(8,128)}) fusion(bf16[4,2,768,768]{3,2,1,0:T(8,128)(2,1)} %bitcast.55), kind=kLoop, calls=%fused_computation.1 | loop fusion | flops 4718592 | bytes 28311552 | tf_op jit(solution)/shard_map/convert_element_type | solution.py:575
  (187 shorter events, 70.2 us)
Async XLA Ops:
  7.2 247.6 %reduce-scatter.7.cloned.1.call-start = ((), (), s32[]{:S(2)}) async-start(), calls=%async_computation.5 | async-start | bytes 2433024
  8.2 13.3 %collective-permute-start.5 = (bf16[96,768]{1,0:T(8,128)(2,1)S(1)}, bf16[96,768]{1,0:T(8,128)(2,1)S(1)}, u32[]{:S(2)}, u32[]{:S(2)}) collective-permute-start(bf16[96,768]{1,0:T(8,128)(2,1)S(1)} %constant_dynamic-slice_fusion), channel_id=1, source_target_pairs={{0,3},{1,0},{2,1},{3,2},{4,7},{5,4},{6,5},{7,6},{8,11},{9,8},{10,9... | collective-permute-start | bytes 442376 | tf_op jit(solution)/shard_map/ppermute | solution.py:415
  13.3 12.5 %collective-permute-start.4 = (bf16[96,768]{1,0:T(8,128)(2,1)S(1)}, bf16[96,768]{1,0:T(8,128)(2,1)S(1)}, u32[]{:S(2)}, u32[]{:S(2)}) collective-permute-start(bf16[96,768]{1,0:T(8,128)(2,1)S(1)} %constant_dynamic-slice_fusion), channel_id=1, source_target_pairs={{0,2},{1,3},{2,0},{3,1},{4,6},{5,7},{6,4},{7,5},{8,10},{9,11},{10,... | collective-permute-start | bytes 442376 | tf_op jit(solution)/shard_map/ppermute | solution.py:415
  13.3 12.5 %collective-permute-start.3 = (bf16[96,768]{1,0:T(8,128)(2,1)S(1)}, bf16[96,768]{1,0:T(8,128)(2,1)S(1)}, u32[]{:S(2)}, u32[]{:S(2)}) collective-permute-start(bf16[96,768]{1,0:T(8,128)(2,1)S(1)} %constant_dynamic-slice_fusion), channel_id=1, source_target_pairs={{0,1},{1,2},{2,3},{3,0},{4,5},{5,6},{6,7},{7,4},{8,9},{9,10},{10,1... | collective-permute-start | bytes 442376 | tf_op jit(solution)/shard_map/ppermute | solution.py:415
  25.8 21.5 %collective-permute-start.6 = (bf16[3,96,768]{2,1,0:T(8,128)(2,1)S(1)}, bf16[3,96,768]{2,1,0:T(8,128)(2,1)S(1)}, u32[]{:S(2)}, u32[]{:S(2)}) collective-permute-start(bf16[3,96,768]{2,1,0:T(8,128)(2,1)S(1)} %pad_maximum_fusion.1), channel_id=1, source_target_pairs={{0,4},{4,0},{8,12},{12,8},{16,20},{20,16},{24,28},{28,24},{1,5},{5... | collective-permute-start | bytes 1327112 | tf_op jit(solution)/shard_map/ppermute | solution.py:420
  38.3 16.9 %collective-permute-start = (bf16[1024,192]{1,0:T(8,128)(2,1)}, bf16[1024,192]{1,0:T(8,128)(2,1)S(1)}, u32[]{:S(2)}, u32[]{:S(2)}) collective-permute-start(bf16[1024,192]{1,0:T(8,128)(2,1)} %get-tuple-element.62.refs_0_), channel_id=1, source_target_pairs={{0,1},{1,2},{2,3},{3,0},{4,5},{5,6},{6,7},{7,4},{8,9},{9,10},{10,1... | collective-permute-start | bytes 1179656 | tf_op jit(solution)/shard_map/ppermute | solution.py:415
  39.1 38.0 %collective-permute-start.1 = (bf16[1024,192]{1,0:T(8,128)(2,1)}, bf16[1024,192]{1,0:T(8,128)(2,1)S(1)}, u32[]{:S(2)}, u32[]{:S(2)}) collective-permute-start(bf16[1024,192]{1,0:T(8,128)(2,1)} %get-tuple-element.62.refs_0_), channel_id=1, source_target_pairs={{0,2},{1,3},{2,0},{3,1},{4,6},{5,7},{6,4},{7,5},{8,10},{9,11},{10,... | collective-permute-start | bytes 1179656 | tf_op jit(solution)/shard_map/ppermute | solution.py:415
  41.1 36.0 %collective-permute-start.2 = (bf16[1024,192]{1,0:T(8,128)(2,1)}, bf16[1024,192]{1,0:T(8,128)(2,1)S(1)}, u32[]{:S(2)}, u32[]{:S(2)}) collective-permute-start(bf16[1024,192]{1,0:T(8,128)(2,1)} %get-tuple-element.62.refs_0_), channel_id=1, source_target_pairs={{0,3},{1,0},{2,1},{3,2},{4,7},{5,4},{6,5},{7,6},{8,11},{9,8},{10,9... | collective-permute-start | bytes 1179656 | tf_op jit(solution)/shard_map/ppermute | solution.py:415
  125.3 23.4 %collective-permute-start.13 = (bf16[256,768]{1,0:T(8,128)(2,1)}, bf16[256,768]{1,0:T(8,128)(2,1)S(1)}, u32[]{:S(2)}, u32[]{:S(2)}) collective-permute-start(bf16[256,768]{1,0:T(8,128)(2,1)} %get-tuple-element.72), channel_id=1, source_target_pairs={{0,1},{1,2},{2,3},{3,0},{4,5},{5,6},{6,7},{7,4},{8,9},{9,10},{10,1... | collective-permute-start | bytes 1179656 | tf_op jit(solution)/shard_map/ppermute | solution.py:415
  136.5 28.0 %collective-permute-start.14 = (bf16[256,768]{1,0:T(8,128)(2,1)}, bf16[256,768]{1,0:T(8,128)(2,1)S(1)}, u32[]{:S(2)}, u32[]{:S(2)}) collective-permute-start(bf16[256,768]{1,0:T(8,128)(2,1)} %get-tuple-element.73), channel_id=1, source_target_pairs={{0,2},{1,3},{2,0},{3,1},{4,6},{5,7},{6,4},{7,5},{8,10},{9,11},{10,... | collective-permute-start | bytes 1179656 | tf_op jit(solution)/shard_map/ppermute | solution.py:415
  138.9 25.6 %collective-permute-start.15 = (bf16[256,768]{1,0:T(8,128)(2,1)}, bf16[256,768]{1,0:T(8,128)(2,1)S(1)}, u32[]{:S(2)}, u32[]{:S(2)}) collective-permute-start(bf16[256,768]{1,0:T(8,128)(2,1)} %get-tuple-element.74), channel_id=1, source_target_pairs={{0,3},{1,0},{2,1},{3,2},{4,7},{5,4},{6,5},{7,6},{8,11},{9,8},{10,9... | collective-permute-start | bytes 1179656 | tf_op jit(solution)/shard_map/ppermute | solution.py:415
  169.9 13.4 %collective-permute-start.16 = (bf16[256,192]{1,0:T(8,128)(2,1)}, bf16[256,192]{1,0:T(8,128)(2,1)S(1)}, u32[]{:S(2)}, u32[]{:S(2)}) collective-permute-start(bf16[256,192]{1,0:T(8,128)(2,1)} %get-tuple-element.76), channel_id=1, source_target_pairs={{0,3},{1,0},{2,1},{3,2},{4,7},{5,4},{6,5},{7,6},{8,11},{9,8},{10,9... | collective-permute-start | bytes 294920 | tf_op jit(solution)/shard_map/ppermute | solution.py:415
  178.8 13.3 %collective-permute-start.17 = (bf16[256,192]{1,0:T(8,128)(2,1)}, bf16[256,192]{1,0:T(8,128)(2,1)S(1)}, u32[]{:S(2)}, u32[]{:S(2)}) collective-permute-start(bf16[256,192]{1,0:T(8,128)(2,1)} %get-tuple-element.77), channel_id=1, source_target_pairs={{0,2},{1,3},{2,0},{3,1},{4,6},{5,7},{6,4},{7,5},{8,10},{9,11},{10,... | collective-permute-start | bytes 294920 | tf_op jit(solution)/shard_map/ppermute | solution.py:415
  180.1 12.0 %collective-permute-start.18 = (bf16[256,192]{1,0:T(8,128)(2,1)}, bf16[256,192]{1,0:T(8,128)(2,1)S(1)}, u32[]{:S(2)}, u32[]{:S(2)}) collective-permute-start(bf16[256,192]{1,0:T(8,128)(2,1)} %get-tuple-element.78), channel_id=1, source_target_pairs={{0,1},{1,2},{2,3},{3,0},{4,5},{5,6},{6,7},{7,4},{8,9},{9,10},{10,1... | collective-permute-start | bytes 294920 | tf_op jit(solution)/shard_map/ppermute | solution.py:415
  214.6 121.1 %reduce-scatter.5.cloned.1.call-start = ((), (), s32[]{:S(2)}) async-start(), calls=%async_computation.3 | async-start | bytes 10616832 | tf_op jit(solution)/shard_map/reduce_scatter | solution.py:571
  230.0 275.3 %all-gather.3.cloned.1.call-start = ((), (), s32[]{:S(2)}) async-start(), calls=%async_computation.2 | async-start | bytes 1327104 | tf_op jit(solution)/shard_map/all_gather | solution.py:646
  256.1 6.9 %collective-permute-start.32 = (bf16[192,96]{1,0:T(8,128)(2,1)S(1)}, bf16[192,96]{1,0:T(8,128)(2,1)S(1)}, u32[]{:S(2)}, u32[]{:S(2)}) collective-permute-start(bf16[192,96]{1,0:T(8,128)(2,1)S(1)} %copy.87), channel_id=1, source_target_pairs={{0,1},{1,2},{2,3},{3,0},{4,5},{5,6},{6,7},{7,4},{8,9},{9,10},{10,1... | collective-permute-start | bytes 110600 | tf_op jit(solution)/shard_map/ppermute | solution.py:415
  265.5 244.3 %all-gather.5.cloned.1.call-start = ((), (), s32[]{:S(2)}) async-start(), calls=%async_computation.4 | async-start | bytes 10616832 | tf_op jit(solution)/shard_map/all_gather | solution.py:572
  335.8 13.3 %collective-permute-start.9 = (bf16[256,768]{1,0:T(8,128)(2,1)}, bf16[256,768]{1,0:T(8,128)(2,1)S(1)}, u32[]{:S(2)}, u32[]{:S(2)}) collective-permute-start(bf16[256,768]{1,0:T(8,128)(2,1)} %get-tuple-element.67), channel_id=1, source_target_pairs={{0,3},{1,0},{2,1},{3,2},{4,7},{5,4},{6,5},{7,6},{8,11},{9,8},{10,9... | collective-permute-start | bytes 1179656 | tf_op jit(solution)/shard_map/ppermute | solution.py:415
  339.2 33.9 %collective-permute-start.8 = (bf16[256,768]{1,0:T(8,128)(2,1)}, bf16[256,768]{1,0:T(8,128)(2,1)S(1)}, u32[]{:S(2)}, u32[]{:S(2)}) collective-permute-start(bf16[256,768]{1,0:T(8,128)(2,1)} %get-tuple-element.66), channel_id=1, source_target_pairs={{0,2},{1,3},{2,0},{3,1},{4,6},{5,7},{6,4},{7,5},{8,10},{9,11},{10,... | collective-permute-start | bytes 1179656 | tf_op jit(solution)/shard_map/ppermute | solution.py:415
  339.2 33.9 %collective-permute-start.7 = (bf16[256,768]{1,0:T(8,128)(2,1)}, bf16[256,768]{1,0:T(8,128)(2,1)S(1)}, u32[]{:S(2)}, u32[]{:S(2)}) collective-permute-start(bf16[256,768]{1,0:T(8,128)(2,1)} %get-tuple-element.65), channel_id=1, source_target_pairs={{0,1},{1,2},{2,3},{3,0},{4,5},{5,6},{6,7},{7,4},{8,9},{9,10},{10,1... | collective-permute-start | bytes 1179656 | tf_op jit(solution)/shard_map/ppermute | solution.py:415
  373.3 85.2 %collective-permute-start.10 = (bf16[256,768]{1,0:T(8,128)(2,1)S(1)}, bf16[256,768]{1,0:T(8,128)(2,1)S(1)}, u32[]{:S(2)}, u32[]{:S(2)}) collective-permute-start(bf16[256,768]{1,0:T(8,128)(2,1)S(1)} %add_convert_fusion.refs_0_), channel_id=1, source_target_pairs={{0,1},{1,2},{2,3},{3,0},{4,5},{5,6},{6,7},{7,4},{8,9},{9,10},{10,1... | collective-permute-start | bytes 1179656 | tf_op jit(solution)/shard_map/ppermute | solution.py:415
  374.3 84.2 %collective-permute-start.11 = (bf16[256,768]{1,0:T(8,128)(2,1)S(1)}, bf16[256,768]{1,0:T(8,128)(2,1)S(1)}, u32[]{:S(2)}, u32[]{:S(2)}) collective-permute-start(bf16[256,768]{1,0:T(8,128)(2,1)S(1)} %add_convert_fusion.refs_0_), channel_id=1, source_target_pairs={{0,2},{1,3},{2,0},{3,1},{4,6},{5,7},{6,4},{7,5},{8,10},{9,11},{10,... | collective-permute-start | bytes 1179656 | tf_op jit(solution)/shard_map/ppermute | solution.py:415
  376.2 28.0 %collective-permute-start.19 = (bf16[256,768]{1,0:T(8,128)(2,1)}, bf16[256,768]{1,0:T(8,128)(2,1)S(1)}, u32[]{:S(2)}, u32[]{:S(2)}) collective-permute-start(bf16[256,768]{1,0:T(8,128)(2,1)} %get-tuple-element.86), channel_id=1, source_target_pairs={{0,1},{1,2},{2,3},{3,0},{4,5},{5,6},{6,7},{7,4},{8,9},{9,10},{10,1... | collective-permute-start | bytes 1179656 | tf_op jit(solution)/shard_map/ppermute | solution.py:415
  377.8 49.6 %collective-permute-start.20 = (bf16[256,768]{1,0:T(8,128)(2,1)}, bf16[256,768]{1,0:T(8,128)(2,1)S(1)}, u32[]{:S(2)}, u32[]{:S(2)}) collective-permute-start(bf16[256,768]{1,0:T(8,128)(2,1)} %get-tuple-element.87), channel_id=1, source_target_pairs={{0,2},{1,3},{2,0},{3,1},{4,6},{5,7},{6,4},{7,5},{8,10},{9,11},{10,... | collective-permute-start | bytes 1179656 | tf_op jit(solution)/shard_map/ppermute | solution.py:415
  379.6 47.8 %collective-permute-start.21 = (bf16[256,768]{1,0:T(8,128)(2,1)}, bf16[256,768]{1,0:T(8,128)(2,1)S(1)}, u32[]{:S(2)}, u32[]{:S(2)}) collective-permute-start(bf16[256,768]{1,0:T(8,128)(2,1)} %get-tuple-element.88), channel_id=1, source_target_pairs={{0,3},{1,0},{2,1},{3,2},{4,7},{5,4},{6,5},{7,6},{8,11},{9,8},{10,9... | collective-permute-start | bytes 1179656 | tf_op jit(solution)/shard_map/ppermute | solution.py:415
  404.2 54.3 %collective-permute-start.12 = (bf16[256,768]{1,0:T(8,128)(2,1)S(1)}, bf16[256,768]{1,0:T(8,128)(2,1)S(1)}, u32[]{:S(2)}, u32[]{:S(2)}) collective-permute-start(bf16[256,768]{1,0:T(8,128)(2,1)S(1)} %add_convert_fusion.refs_0_), channel_id=1, source_target_pairs={{0,3},{1,0},{2,1},{3,2},{4,7},{5,4},{6,5},{7,6},{8,11},{9,8},{10,9... | collective-permute-start | bytes 1179656 | tf_op jit(solution)/shard_map/ppermute | solution.py:415
  442.2 26.7 %collective-permute-start.28 = (f32[6,768]{1,0:T(8,128)S(1)}, f32[6,768]{1,0:T(8,128)S(1)}, u32[]{:S(2)}, u32[]{:S(2)}) collective-permute-start(f32[6,768]{1,0:T(8,128)S(1)} %slice.115), channel_id=1, source_target_pairs={{0,1},{1,0},{2,3},{3,2},{4,5},{5,4},{6,7},{7,6},{8,9},{9,8},{10,11... | collective-permute-start | bytes 55304 | tf_op jit(solution)/shard_map/ppermute | solution.py:420
  462.7 37.8 %collective-permute-start.22 = (bf16[256,768]{1,0:T(8,128)(2,1)S(1)}, bf16[256,768]{1,0:T(8,128)(2,1)S(1)}, u32[]{:S(2)}, u32[]{:S(2)}) collective-permute-start(bf16[256,768]{1,0:T(8,128)(2,1)S(1)} %copy-done.9), channel_id=1, source_target_pairs={{0,1},{1,2},{2,3},{3,0},{4,5},{5,6},{6,7},{7,4},{8,9},{9,10},{10,1... | collective-permute-start | bytes 1179656 | tf_op jit(solution)/shard_map/ppermute | solution.py:415
  462.7 37.7 %collective-permute-start.23 = (bf16[256,768]{1,0:T(8,128)(2,1)S(1)}, bf16[256,768]{1,0:T(8,128)(2,1)S(1)}, u32[]{:S(2)}, u32[]{:S(2)}) collective-permute-start(bf16[256,768]{1,0:T(8,128)(2,1)S(1)} %copy-done.9), channel_id=1, source_target_pairs={{0,2},{1,3},{2,0},{3,1},{4,6},{5,7},{6,4},{7,5},{8,10},{9,11},{10,... | collective-permute-start | bytes 1179656 | tf_op jit(solution)/shard_map/ppermute | solution.py:415
  466.0 34.5 %collective-permute-start.24 = (bf16[256,768]{1,0:T(8,128)(2,1)S(1)}, bf16[256,768]{1,0:T(8,128)(2,1)S(1)}, u32[]{:S(2)}, u32[]{:S(2)}) collective-permute-start(bf16[256,768]{1,0:T(8,128)(2,1)S(1)} %copy-done.9), channel_id=1, source_target_pairs={{0,3},{1,0},{2,1},{3,2},{4,7},{5,4},{6,5},{7,6},{8,11},{9,8},{10,9... | collective-permute-start | bytes 1179656 | tf_op jit(solution)/shard_map/ppermute | solution.py:415
  468.9 30.3 %collective-permute-start.29 = (f32[6,768]{1,0:T(8,128)S(1)}, f32[6,768]{1,0:T(8,128)S(1)}, u32[]{:S(2)}, u32[]{:S(2)}) collective-permute-start(f32[6,768]{1,0:T(8,128)S(1)} %slice_add_fusion), channel_id=1, source_target_pairs={{0,2},{1,3},{2,0},{3,1},{4,6},{5,7},{6,4},{7,5},{8,10},{9,11},{10,... | collective-permute-start | bytes 55304 | tf_op jit(solution)/shard_map/ppermute | solution.py:420
  (41 other events, 787.0 us)
Sparse Core Ops, SparseCore 0:
  214.7 40.0 reduce-scatter.6
  259.3 76.4 reduce-scatter.4
  337.8 24.0 all-gather.2
  363.8 58.8 all-gather.4
